TPU v7x, 768 devices: a whole 4x8x12 slice. The times are simulated.
768 devices in a mesh: xy: 32 (over x, y), gz: 24 (over z, core).
Axes of the slice: x: 4, y: 8, z: 12, core: 2. Of those that a mesh axis runs over, the one named last changes fastest.
Arguments:
- velocity: float32 [3, 96, 1024, 1024], P(None, 'gz', 'xy'), may hold values from -6 to 6
- magnetic: float32 [3, 48, 512, 512], P(None, 'gz', 'xy'), may hold values from -6 to 6
- slot_block_table: int32 [1024], P('xy'), may hold values from 0 to 1023, as said below
Outputs:
- updated_fine_velocity: float32 [3, 96, 1024, 1024], P(None, 'gz', 'xy')
- magnetic_next: float32 [3, 48, 512, 512], P(None, 'gz', 'xy')
Inputs may be any that keep to these rules, and one draw needn't show every extreme that they name: `slot_block_table`: each block number appears in one slot; the 32 slots of one device along xy hold exactly 1 block of every block row.
All inputs are finite; a program needn't handle non-finite values.
Results may differ from a plain program's by a relative error of at most 0.00005.
Values sent between devices are 32-bit elements; how exact they have to be, the bound alone decides.
A program may use at most 64 MiB of HBM per device.

v0:
```python
import jax
import jax.numpy as jnp
from jax import lax
from jax.sharding import PartitionSpec as P

BLOCK_EDGE = 32


def extended(value, sides, width):
    edges = {}
    for axis, dim in sides:
        size, length = (lax.axis_size(axis), value.shape[dim])
        up = [(i, (i + 1) % size) for i in range(size)]
        last = lax.slice_in_dim(value, length - width, length, axis=dim)
        first = lax.slice_in_dim(value, 0, width, axis=dim)
        edges[dim] = (
            lax.ppermute(last, axis, up),
            lax.ppermute(first, axis, [(b, a) for a, b in up]),
        )
    done = []
    for _, dim in sides:
        low, high = edges[dim]
        around = [(width, width) if d in done else (0, 0) for d in range(value.ndim)]
        value = jnp.concatenate([jnp.pad(low, around), value, jnp.pad(high, around)], axis=dim)
        done.append(dim)
    return value


def restrict(fine, blk):
    half_width = blk // 2
    s = fine.shape
    v = fine.reshape(s[0], s[1] // 2, 2, s[2], half_width, 2, half_width, 2)
    return (jnp.sum(v, axis=(2, 5, 7)) * 0.125).reshape(
        s[0], s[1] // 2, s[2], half_width * half_width
    )


def inner(padded):
    return padded[:, 1:-1, 1:-1]


def along_z(padded):
    return (padded[:, 2:, 1:-1] - padded[:, :-2, 1:-1]) * 0.5


def along_y(padded):
    return (padded[:, 1:-1, 2:] - padded[:, 1:-1, :-2]) * 0.5


def along_x(padded):
    middle = inner(padded)
    return (jnp.roll(middle, -1, 3) - jnp.roll(middle, 1, 3)) * 0.5


def curl_padded(padded):
    dzv = along_z(padded)
    dyv = along_y(padded)
    dxv = along_x(padded)
    return jnp.stack([dyv[2] - dzv[1], dzv[0] - dxv[2], dxv[1] - dyv[0]])


def cross(a, b):
    return jnp.stack(
        [a[1] * b[2] - a[2] * b[1], a[2] * b[0] - a[0] * b[2], a[0] * b[1] - a[1] * b[0]]
    )


def laplace_padded(padded):
    middle = inner(padded)
    total = padded[:, 2:, 1:-1] + padded[:, :-2, 1:-1] + padded[:, 1:-1, 2:] + padded[:, 1:-1, :-2]
    return total + jnp.roll(middle, 1, 3) + jnp.roll(middle, -1, 3) - 6.0 * middle


def split_into_tiles(magnetic_state, coarse_depth_index, half_width, slot_count):
    return (
        magnetic_state.reshape(
            magnetic_state.shape[0], coarse_depth_index, half_width, slot_count, half_width
        )
        .transpose(0, 1, 3, 2, 4)
        .reshape(magnetic_state.shape[0], coarse_depth_index, slot_count, half_width * half_width)
    )


def assemble_from_tiles(tile_stack, coarse_depth_index, half_width, slot_count):
    return (
        tile_stack.reshape(
            tile_stack.shape[0], coarse_depth_index, slot_count, half_width, half_width
        )
        .transpose(0, 1, 3, 2, 4)
        .reshape(tile_stack.shape[0], coarse_depth_index, half_width, slot_count * half_width)
    )


def body(velocity, magnetic, slot_block_table):
    half_width = BLOCK_EDGE // 2
    slot_count = velocity.shape[2]
    coarse_depth_index = velocity.shape[1] // 2
    column_indices = slot_block_table % slot_count
    sorted_positions = jnp.argsort(slot_block_table)
    dispatched_columns = column_indices[sorted_positions].reshape(1, 1, slot_count, 1)
    ordered = velocity[:, :, sorted_positions]
    got, received_columns = (
        lax.all_to_all(
            restrict(ordered, BLOCK_EDGE), "xy", split_axis=2, concat_axis=2, tiled=True
        ),
        lax.all_to_all(dispatched_columns, "xy", split_axis=2, concat_axis=2, tiled=True),
    )
    column_listing = received_columns.reshape(slot_count)
    grouped_by_column = got[:, :, jnp.argsort(column_listing)]
    coarse_flow_field = assemble_from_tiles(
        grouped_by_column, coarse_depth_index, half_width, slot_count
    )
    emf = cross(coarse_flow_field, magnetic)
    stacked = jnp.concatenate([magnetic, emf], axis=0)
    padded = extended(stacked, (("xy", 2), ("gz", 1)), 1)
    field_pad = padded[0:3]
    current = curl_padded(field_pad)
    magnetic_next = magnetic + 0.1 * (curl_padded(padded[3:6]) + 0.5 * laplace_padded(field_pad))
    lorentz_force = cross(current, magnetic)
    returned_back_tiles = split_into_tiles(
        lorentz_force, coarse_depth_index, half_width, slot_count
    )[:, :, column_listing]
    returned = lax.all_to_all(returned_back_tiles, "xy", split_axis=2, concat_axis=2, tiled=True)
    blocks_per_slot = returned[:, :, jnp.argsort(sorted_positions)]
    widened_tiles = jnp.broadcast_to(
        blocks_per_slot.reshape(3, coarse_depth_index, 1, slot_count, half_width, 1, half_width, 1),
        (3, coarse_depth_index, 2, slot_count, half_width, 2, half_width, 2),
    )
    updated_fine_velocity = velocity + 0.1 * widened_tiles.reshape(
        3, coarse_depth_index * 2, slot_count, BLOCK_EDGE * BLOCK_EDGE
    )
    return (updated_fine_velocity, magnetic_next)


def solution(mesh):
    return jax.shard_map(
        body,
        mesh=mesh,
        in_specs=(P(None, "gz", "xy", None), P(None, "gz", "xy", None), P("xy")),
        out_specs=(P(None, "gz", "xy", None), P(None, "gz", "xy", None)),
        check_vma=False,
    )
```

profile of v0, /device:TPU:8, one launch (start us, length us, event | category | flops | bytes accessed | tf_op | source)
XLA Modules:
  0.0 125.6 jit_solution(15834562630646758362)
XLA Ops:
  0.6 0.8 and_select_fusion
  1.4 2.3 %sort.45 = (s32[32]{0:T(128)}, s32[32]{0:T(128)S(1)}) sort(s32[32]{0:T(128)} %param.5, s32[32]{0:T(128)S(1)} %iota.10), dimensions={0}, to_apply=%region_0.1 | sort | flops 160 | bytes 512 | tf_op jit(solution)/shard_map/jit(argsort)/sort | solution.py:99
  3.7 0.7 gather_fusion.1
  4.4 0.7 copy.33
  5.1 12.9 %all-to-all-start.1 = ((s32[1,1,32,1]{3,1,0,2:T(1,128)}), s32[1,1,32,1]{3,1,0,2:T(1,128)S(1)}, u32[]{:S(2)}, u32[]{:S(2)}) async-start(s32[1,1,32,1]{3,1,0,2:T(1,128)} %copy.33), calls=%async_computation.1 | async-start | bytes 32768 | tf_op jit(solution)/shard_map/all_to_all | solution.py:106
  18.1 1.5 %fusion.13 = (f32[3,2,16,1]{3,2,1,0:T(8,128)}, f32[3,2,16,1]{3,2,1,0:T(8,128)}) fusion(f32[3,2,16,512]{3,2,1,0:T(8,128)} %param.4), kind=kLoop, calls=%fused_computation.70 | loop fusion | bytes 1536 | tf_op jit(solution)/shard_map/jit(_roll_static)/slice | solution.py:52
  19.6 1.1 fusion.12
  20.7 1.6 %sort.47 = (s32[32]{0:T(128)}, s32[32]{0:T(128)S(1)}) sort(s32[32]{0:T(128)S(1)} %get-tuple-element.5, s32[32]{0:T(128)S(1)} %iota.12), dimensions={0}, to_apply=%region_3.4 | sort | flops 160 | bytes 512 | tf_op jit(solution)/shard_map/jit(argsort)/sort | solution.py:124
  22.4 0.5 compare_select_fusion
  22.9 3.0 %gather_fusion = f32[32,3,4,1024]{3,0,2,1:T(8,128)S(1)} fusion(f32[3,4,32,1024]{3,2,1,0:T(8,128)S(1)} %copy-done, s32[1024]{0:T(1024)} %copy-done.19), kind=kCustom, calls=%fused_computation | custom fusion | bytes 3145856 | tf_op jit(solution)/shard_map/gather | solution.py:101
  25.8 4.0 %copy.31 = f32[3,4,32,1024]{2,3,1,0:T(8,128)} copy(f32[3,4,32,1024]{3,2,1,0:T(8,128)S(1)} %bitcast.34) | data formatting | bytes 3145728 | tf_op jit(solution)/shard_map/gather | solution.py:101
  29.8 7.3 %reduce_sum.9 = f32[3,2,32,16,16]{2,4,3,1,0:T(8,128)S(1)} reduce(f32[3,2,2,32,16,2,16,2]{3,7,6,5,4,2,1,0:T(2,128)} %bitcast.32, f32[]{:T(128)} %constant.11.clone.1), dimensions={2,5,7}, to_apply=%region_1.2 | reduce | flops 344064 | bytes 1769476 | tf_op jit(solution)/shard_map/reduce_sum | solution.py:33
  37.2 0.7 copy-done.11
  38.1 0.6 pad_clamp_fusion
  38.7 4.0 %copy.43 = f32[3,4,32,1024]{2,3,1,0:T(8,128)} copy(f32[3,4,32,1024]{3,2,1,0:T(8,128)S(1)} %copy-done) | data formatting | bytes 3145728 | tf_op args[0]
  42.7 0.9 copy.32
  43.6 9.9 %all-to-all-start = ((f32[3,2,32,256]{3,1,0,2:T(2,128)}), f32[3,2,32,256]{3,1,0,2:T(2,128)S(1)}, u32[]{:S(2)}, u32[]{:S(2)}) async-start(f32[3,2,32,256]{3,1,0,2:T(2,128)} %copy.32), calls=%async_computation | async-start | bytes 393216 | tf_op jit(solution)/shard_map/all_to_all | solution.py:103
  53.5 0.7 reduce
  54.2 1.6 %sort.46 = (s32[32]{0:T(128)}, s32[32]{0:T(128)S(1)}) sort(s32[32]{0:T(128)S(1)} %reduce, s32[32]{0:T(128)S(1)} %iota.11), dimensions={0}, to_apply=%region_2.3 | sort | flops 160 | bytes 512 | tf_op jit(solution)/shard_map/jit(argsort)/sort | solution.py:109
  55.8 8.2 %all-to-all-done = f32[3,2,32,256]{3,1,0,2:T(2,128)S(1)} async-done(((f32[3,2,32,256]{3,1,0,2:T(2,128)}), f32[3,2,32,256]{3,1,0,2:T(2,128)S(1)}, u32[]{:S(2)}, u32[]{:S(2)}) %all-to-all-start) | async-done | bytes 196640 | tf_op jit(solution)/shard_map/all_to_all | solution.py:103
  64.0 0.8 gather_fusion.2
  64.8 0.3 copy.35
  65.2 0.2 copy.37
  65.4 0.3 squeeze.7
  65.7 0.2 copy.38
  65.9 0.3 squeeze.8
  66.2 0.2 copy.36
  66.4 0.3 squeeze.6
  66.8 2.3 %collective-permute-start = (f32[6,2,1,512]{3,2,1,0:T(1,128)S(1)}, f32[6,2,1,512]{3,2,1,0:T(1,128)S(1)}, u32[]{:S(2)}, u32[]{:S(2)}) collective-permute-start(f32[6,2,1,512]{3,2,1,0:T(1,128)S(1)} %get-tuple-element.26), channel_id=1, source_target_pairs={{0,24},{24,48},{48,72},{72,96},{96,120},{120,144},{144,168},{168,1... | collective-permute-start | bytes 73736 | tf_op jit(solution)/shard_map/ppermute | solution.py:17
  69.1 3.6 %collective-permute-start.1 = (f32[6,2,1,512]{3,2,1,0:T(1,128)S(1)}, f32[6,2,1,512]{3,2,1,0:T(1,128)S(1)}, u32[]{:S(2)}, u32[]{:S(2)}) collective-permute-start(f32[6,2,1,512]{3,2,1,0:T(1,128)S(1)} %get-tuple-element.27), channel_id=1, source_target_pairs={{24,0},{48,24},{72,48},{96,72},{120,96},{144,120},{168,144},{192,1... | collective-permute-start | bytes 73736 | tf_op jit(solution)/shard_map/ppermute | solution.py:18
  72.7 6.7 %collective-permute-start.2 = (f32[6,1,16,512]{3,2,1,0:T(8,128)S(1)}, f32[6,1,16,512]{3,2,1,0:T(8,128)S(1)}, u32[]{:S(2)}, u32[]{:S(2)}) collective-permute-start(f32[6,1,16,512]{3,2,1,0:T(8,128)S(1)} %get-tuple-element.24), channel_id=1, source_target_pairs={{1,0},{2,1},{3,2},{4,3},{5,4},{6,5},{7,6},{8,7},{9,8},{10,9},{11,1... | collective-permute-start | bytes 589832 | tf_op jit(solution)/shard_map/ppermute | solution.py:18
  79.6 0.7 fusion.2
  80.4 2.1 %collective-permute-done.2 = f32[6,1,16,512]{3,2,1,0:T(8,128)S(1)} collective-permute-done((f32[6,1,16,512]{3,2,1,0:T(8,128)S(1)}, f32[6,1,16,512]{3,2,1,0:T(8,128)S(1)}, u32[]{:S(2)}, u32[]{:S(2)}) %collective-permute-start.2) | collective-permute-done | bytes 196640 | tf_op jit(solution)/shard_map/ppermute | solution.py:18
  82.6 3.3 %collective-permute-done.3 = f32[6,1,16,512]{3,2,1,0:T(8,128)S(1)} collective-permute-done((f32[6,1,16,512]{3,2,1,0:T(8,128)S(1)}, f32[6,1,16,512]{3,2,1,0:T(8,128)S(1)}, u32[]{:S(2)}, u32[]{:S(2)}) %collective-permute-start.3) | collective-permute-done | bytes 196640 | tf_op jit(solution)/shard_map/ppermute | solution.py:17
  86.1 0.9 copy-done.3
  87.0 0.9 fusion
  88.6 0.2 maximum_bitcast_fusion
  88.9 0.5 copy.39
  89.4 0.3 copy.40
  89.7 1.4 %gather_fusion.3 = f32[32,3,2,256]{3,2,1,0:T(2,128)} fusion(f32[3,2,32,256]{3,1,2,0:T(2,128)S(1)} %copy.40, s32[1024]{0:T(1024)S(1)} %pad_clamp_fusion.1), kind=kCustom, calls=%fused_computation.3 | custom fusion | bytes 393344 | tf_op jit(solution)/shard_map/gather | solution.py:120
  91.1 7.5 %all-to-all-start.2 = ((f32[3,2,32,256]{3,1,0,2:T(2,128)}), f32[3,2,32,256]{3,1,0,2:T(2,128)S(1)}, u32[]{:S(2)}, u32[]{:S(2)}) async-start(f32[3,2,32,256]{3,1,0,2:T(2,128)} %bitcast.11), calls=%async_computation.2 | async-start | bytes 393216 | tf_op jit(solution)/shard_map/all_to_all | solution.py:123
  98.8 1.9 %fusion.5 = f32[3,2,16,512]{3,2,1,0:T(8,128)} fusion(f32[3,2,16,512]{3,2,1,0:T(8,128)S(1)} %copy-done.1, f32[1,2,16,512]{3,2,1,0:T(8,128)S(1)} %get-tuple-element.32, f32[1,2,16,512]{3,2,1,0:T(8,128)S(1)} %get-tuple-element.33, f32[1,2,16,512]{3,2,1,0:T(8,128)S(1)} %get-tuple-element.31, f32[6,3,18,512]{3,2,1,0:T(8,128)} %copy-done.3, ...), kind=kLoop, calls=%fused_computation.33 | loop fusion | flops 1130496 | bytes 1622016 | tf_op jit(solution)/shard_map/add | solution.py:118
  100.7 8.5 %all-to-all-done.2 = f32[3,2,32,256]{3,1,0,2:T(2,128)S(1)} async-done(((f32[3,2,32,256]{3,1,0,2:T(2,128)}), f32[3,2,32,256]{3,1,0,2:T(2,128)S(1)}, u32[]{:S(2)}, u32[]{:S(2)}) %all-to-all-start.2) | async-done | bytes 196640 | tf_op jit(solution)/shard_map/all_to_all | solution.py:123
  109.3 0.9 gather_fusion.4
  110.3 0.3 copy.42
  110.6 3.2 %broadcast_in_dim.19 = f32[3,2,2,32,16,2,16,2]{3,7,6,5,4,2,1,0:T(2,128)S(1)} broadcast(f32[3,2,32,16,16]{2,4,3,1,0:T(8,128)S(1)} %bitcast.35), dimensions={0,1,3,4,6} | broadcast | bytes 1769472 | tf_op jit(solution)/shard_map/broadcast_in_dim | solution.py:125
  113.8 6.3 %add.59 = f32[3,4,32,1024]{2,3,1,0:T(8,128)} add(f32[3,4,32,1024]{2,3,1,0:T(8,128)} %copy.43, f32[3,4,32,1024]{2,3,1,0:T(8,128)S(1)} %bitcast.33) | non-fusion elementwise | flops 393216 | bytes 4718592 | tf_op jit(solution)/shard_map/add | solution.py:129
  120.1 5.5 %copy.44 = f32[3,4,32,1024]{3,2,1,0:T(8,128)} copy(f32[3,4,32,1024]{2,3,1,0:T(8,128)} %add.59) | data formatting | bytes 3145728
  (72 shorter events, 1.9 us)
Async XLA Ops:
  0.6 22.3 %copy-start = (f32[3,4,32,1024]{3,2,1,0:T(8,128)S(1)}, f32[3,4,32,1024]{3,2,1,0:T(8,128)}, u32[]{:S(2)}) copy-start(f32[3,4,32,1024]{3,2,1,0:T(8,128)} %param.3) | copy-start | bytes 4718596
  3.7 18.7 %copy-start.19 = (s32[1024]{0:T(1024)}, s32[1024]{0:T(1024)S(1)}, u32[]{:S(2)}) copy-start(s32[1024]{0:T(1024)S(1)} %pad_clamp_fusion.3) | copy-start | bytes 12292
  5.1 38.5 %all-to-all-start.1 = ((s32[1,1,32,1]{3,1,0,2:T(1,128)}), s32[1,1,32,1]{3,1,0,2:T(1,128)S(1)}, u32[]{:S(2)}, u32[]{:S(2)}) async-start(s32[1,1,32,1]{3,1,0,2:T(1,128)} %copy.33), calls=%async_computation.1 | async-start | bytes 32768 | tf_op jit(solution)/shard_map/all_to_all | solution.py:106
  20.7 16.5 %copy-start.4 = (f32[3,2,16,511]{3,2,1,0:T(8,128)}, f32[3,2,16,511]{3,2,1,0:T(8,128)S(1)}, u32[]{:S(2)}) copy-start(f32[3,2,16,511]{3,2,1,0:T(8,128)S(1)} %get-tuple-element.40) | copy-start | bytes 588676
  20.7 16.5 %copy-start.6 = (f32[3,2,16,511]{3,2,1,0:T(8,128)}, f32[3,2,16,511]{3,2,1,0:T(8,128)S(1)}, u32[]{:S(2)}) copy-start(f32[3,2,16,511]{3,2,1,0:T(8,128)S(1)} %get-tuple-element.41) | copy-start | bytes 588676
  37.1 0.8 copy-start.11
  37.1 0.8 copy-start.13
  37.1 0.9 copy-start.20
  43.6 20.4 %all-to-all-start = ((f32[3,2,32,256]{3,1,0,2:T(2,128)}), f32[3,2,32,256]{3,1,0,2:T(2,128)S(1)}, u32[]{:S(2)}, u32[]{:S(2)}) async-start(f32[3,2,32,256]{3,1,0,2:T(2,128)} %copy.32), calls=%async_computation | async-start | bytes 393216 | tf_op jit(solution)/shard_map/all_to_all | solution.py:103
  65.4 1.3 %copy-start.1 = (f32[3,2,16,512]{3,2,1,0:T(8,128)S(1)}, f32[3,2,16,512]{3,2,1,0:T(8,128)}, u32[]{:S(2)}) copy-start(f32[3,2,16,512]{3,2,1,0:T(8,128)} %param.4) | copy-start | bytes 589828
  66.8 12.6 %collective-permute-start = (f32[6,2,1,512]{3,2,1,0:T(1,128)S(1)}, f32[6,2,1,512]{3,2,1,0:T(1,128)S(1)}, u32[]{:S(2)}, u32[]{:S(2)}) collective-permute-start(f32[6,2,1,512]{3,2,1,0:T(1,128)S(1)} %get-tuple-element.26), channel_id=1, source_target_pairs={{0,24},{24,48},{48,72},{72,96},{96,120},{120,144},{144,168},{168,1... | collective-permute-start | bytes 73736 | tf_op jit(solution)/shard_map/ppermute | solution.py:17
  69.1 10.3 %collective-permute-start.1 = (f32[6,2,1,512]{3,2,1,0:T(1,128)S(1)}, f32[6,2,1,512]{3,2,1,0:T(1,128)S(1)}, u32[]{:S(2)}, u32[]{:S(2)}) collective-permute-start(f32[6,2,1,512]{3,2,1,0:T(1,128)S(1)} %get-tuple-element.27), channel_id=1, source_target_pairs={{24,0},{48,24},{72,48},{96,72},{120,96},{144,120},{168,144},{192,1... | collective-permute-start | bytes 73736 | tf_op jit(solution)/shard_map/ppermute | solution.py:18
  72.7 9.9 %collective-permute-start.2 = (f32[6,1,16,512]{3,2,1,0:T(8,128)S(1)}, f32[6,1,16,512]{3,2,1,0:T(8,128)S(1)}, u32[]{:S(2)}, u32[]{:S(2)}) collective-permute-start(f32[6,1,16,512]{3,2,1,0:T(8,128)S(1)} %get-tuple-element.24), channel_id=1, source_target_pairs={{1,0},{2,1},{3,2},{4,3},{5,4},{6,5},{7,6},{8,7},{9,8},{10,9},{11,1... | collective-permute-start | bytes 589832 | tf_op jit(solution)/shard_map/ppermute | solution.py:18
  79.4 6.5 %collective-permute-start.3 = (f32[6,1,16,512]{3,2,1,0:T(8,128)S(1)}, f32[6,1,16,512]{3,2,1,0:T(8,128)S(1)}, u32[]{:S(2)}, u32[]{:S(2)}) collective-permute-start(f32[6,1,16,512]{3,2,1,0:T(8,128)S(1)} %get-tuple-element.25), channel_id=1, source_target_pairs={{0,1},{1,2},{2,3},{3,4},{4,5},{5,6},{6,7},{7,8},{8,9},{9,10},{10,1... | collective-permute-start | bytes 589832 | tf_op jit(solution)/shard_map/ppermute | solution.py:17
  79.4 6.7 %copy-start.15 = (f32[6,2,1,512]{3,2,1,0:T(1,128)}, f32[6,2,1,512]{3,2,1,0:T(1,128)S(1)}, u32[]{:S(2)}) copy-start(f32[6,2,1,512]{3,2,1,0:T(1,128)S(1)} %collective-permute-done) | copy-start | bytes 73732
  79.4 6.7 %copy-start.17 = (f32[6,2,1,512]{3,2,1,0:T(1,128)}, f32[6,2,1,512]{3,2,1,0:T(1,128)S(1)}, u32[]{:S(2)}) copy-start(f32[6,2,1,512]{3,2,1,0:T(1,128)S(1)} %collective-permute-done.1) | copy-start | bytes 73732
  86.1 0.9 copy-start.3
  86.1 2.1 %copy-start.2 = (f32[6,3,18,512]{3,2,1,0:T(8,128)}, f32[6,3,18,512]{3,2,1,0:T(8,128)S(1)}, u32[]{:S(2)}) copy-start(f32[6,3,18,512]{3,2,1,0:T(8,128)S(1)} %get-tuple-element.22) | copy-start | bytes 1990660
  88.9 9.8 %copy-start.8 = (f32[3,2,16,512]{3,2,1,0:T(8,128)S(1)}, f32[3,2,16,512]{3,2,1,0:T(8,128)}, u32[]{:S(2)}) copy-start(f32[3,2,16,512]{3,2,1,0:T(8,128)} %get-tuple-element.14) | copy-start | bytes 589828
  88.9 9.8 %copy-start.9 = (f32[3,2,16,512]{3,2,1,0:T(8,128)S(1)}, f32[3,2,16,512]{3,2,1,0:T(8,128)}, u32[]{:S(2)}) copy-start(f32[3,2,16,512]{3,2,1,0:T(8,128)} %get-tuple-element.44) | copy-start | bytes 589828
  88.9 9.8 %copy-start.10 = (f32[3,2,16,512]{3,2,1,0:T(8,128)S(1)}, f32[3,2,16,512]{3,2,1,0:T(8,128)}, u32[]{:S(2)}) copy-start(f32[3,2,16,512]{3,2,1,0:T(8,128)} %fusion.2) | copy-start | bytes 589828
  89.4 9.4 %copy-start.5 = (f32[3,2,16,511]{3,2,1,0:T(8,128)S(1)}, f32[3,2,16,511]{3,2,1,0:T(8,128)}, u32[]{:S(2)}) copy-start(f32[3,2,16,511]{3,2,1,0:T(8,128)} %copy-done.4) | copy-start | bytes 588676
  89.4 9.4 %copy-start.7 = (f32[3,2,16,511]{3,2,1,0:T(8,128)S(1)}, f32[3,2,16,511]{3,2,1,0:T(8,128)}, u32[]{:S(2)}) copy-start(f32[3,2,16,511]{3,2,1,0:T(8,128)} %copy-done.6) | copy-start | bytes 588676
  89.4 9.4 %copy-start.12 = (f32[3,2,16,1]{3,2,1,0:T(8,128)S(1)}, f32[3,2,16,1]{3,2,1,0:T(8,128)}, u32[]{:S(2)}) copy-start(f32[3,2,16,1]{3,2,1,0:T(8,128)} %get-tuple-element.42) | copy-start | bytes 1156
  89.4 9.4 %copy-start.14 = (f32[3,2,16,1]{3,2,1,0:T(8,128)S(1)}, f32[3,2,16,1]{3,2,1,0:T(8,128)}, u32[]{:S(2)}) copy-start(f32[3,2,16,1]{3,2,1,0:T(8,128)} %get-tuple-element.43) | copy-start | bytes 1156
  89.4 9.4 %copy-start.16 = (f32[6,2,1,512]{3,2,1,0:T(1,128)S(1)}, f32[6,2,1,512]{3,2,1,0:T(1,128)}, u32[]{:S(2)}) copy-start(f32[6,2,1,512]{3,2,1,0:T(1,128)} %copy-done.15) | copy-start | bytes 73732
  89.4 9.4 %copy-start.18 = (f32[6,2,1,512]{3,2,1,0:T(1,128)S(1)}, f32[6,2,1,512]{3,2,1,0:T(1,128)}, u32[]{:S(2)}) copy-start(f32[6,2,1,512]{3,2,1,0:T(1,128)} %copy-done.17) | copy-start | bytes 73732
  91.1 18.1 %all-to-all-start.2 = ((f32[3,2,32,256]{3,1,0,2:T(2,128)}), f32[3,2,32,256]{3,1,0,2:T(2,128)S(1)}, u32[]{:S(2)}, u32[]{:S(2)}) async-start(f32[3,2,32,256]{3,1,0,2:T(2,128)} %bitcast.11), calls=%async_computation.2 | async-start | bytes 393216 | tf_op jit(solution)/shard_map/all_to_all | solution.py:123
where the time goes:
time: 126 us
  starting transfers between devices  42.9 us (34%)
  local copies, waits for them, and re-layouts  33.1 us (26%)
  other arithmetic  26.2 us (21%)
  waiting for transfers between devices  22.2 us (18%)
    all_to_all x1, starting transfers between devices, body(): lax.all_to_all(dispatched_columns, 'xy', split_axis=2, concat_axis=2, til...  12.9 us
    unnamed x44, local copies, waits for them, and re-layouts  11.2 us
    ppermute x2, starting transfers between devices, extended(): lax.ppermute(first, axis, [(b, a) for a, b in up])  10.2 us
    all_to_all x1, starting transfers between devices, body(): lax.all_to_all(restrict(ordered, BLOCK_EDGE), 'xy', split_axis=2, concat_...  9.9 us
    all_to_all x1, waiting for transfers between devices, body(): lax.all_to_all(returned_back_tiles, 'xy', split_axis=2, concat_axis=2, ti...  8.54 us
    all_to_all x1, waiting for transfers between devices, body(): lax.all_to_all(restrict(ordered, BLOCK_EDGE), 'xy', split_axis=2, concat_...  8.17 us
    all_to_all x1, starting transfers between devices, body(): lax.all_to_all(returned_back_tiles, 'xy', split_axis=2, concat_axis=2, ti...  7.52 us
    reduce_sum x1, other arithmetic, restrict(): jnp.sum(v, axis=(2, 5, 7)) * 0.125  7.27 us
  transfers between devices with their start and end apart: 7, of which 4 were waited for; matrix products, arithmetic and copies ran while one was open for 24% of the time, Pallas kernels for 0%

commit v1 on v0

v1 whole, which is shorter than its diff:
```python
import functools

import jax
import jax.numpy as jnp
from jax import lax
from jax.experimental import pallas as pl
from jax.experimental.pallas import tpu as pltpu
from jax.sharding import PartitionSpec as P

MESH = pl.DeviceIdType.MESH
LANES = 128
EDGE = 16
ROWS = 12


def halves(value):
    high = value.astype(jnp.bfloat16)
    return high, (value - high.astype(jnp.float32)).astype(jnp.bfloat16)


def stacked_halves(value):
    return jnp.concatenate(halves(value), axis=0)


def dot(a, b):
    return jnp.dot(a, b, preferred_element_type=jnp.float32)


def iota(shape, dim):
    return lax.broadcasted_iota(jnp.int32, shape, dim)


def one_hot(condition):
    return jnp.where(condition, 1.0, 0.0)


def turn_chunks(tile):
    t, m = iota((8, LANES), 0), iota((8, LANES), 1) // EDGE
    skewed = pltpu.roll(tile, 0, 1, stride=EDGE, stride_axis=0)
    picked = jnp.take_along_axis(skewed, (m + t) & 7, axis=0)
    return pltpu.roll(picked, 0, 1, stride=EDGE, stride_axis=0)


def blocks_to_grid(half_rows, n):
    return jnp.concatenate(
        [
            jnp.concatenate(
                [turn_chunks(rows[8 * g : 8 * g + 8]) for g in range(n // 8)], axis=1
            )
            for rows in half_rows
        ],
        axis=0,
    )


def grid_to_blocks(plane, n):
    return [
        jnp.concatenate(
            [
                turn_chunks(plane[8 * h : 8 * h + 8, LANES * g : LANES * g + LANES])
                for g in range(n // 8)
            ],
            axis=0,
        )
        for h in range(2)
    ]


def shift_x(plane):
    width = plane.shape[1]
    return (pltpu.roll(plane, width - 1, 1), pltpu.roll(plane, 1, 1))


def shift_y(plane, low, high):
    y = iota(plane.shape, 0)
    return (
        jnp.where(y == EDGE - 1, high, pltpu.roll(plane, EDGE - 1, 0)),
        jnp.where(y == 0, low, pltpu.roll(plane, 1, 0)),
    )


def central(pair):
    return (pair[0] - pair[1]) * 0.5


def cross(a, b):
    return [
        a[1] * b[2] - a[2] * b[1],
        a[2] * b[0] - a[0] * b[2],
        a[0] * b[1] - a[1] * b[0],
    ]


def kernel(
    cols, rows, depth,
    vel, mag, table, vel_out, mag_out,
    fine, field, ids_send, ids, v_send, v_got, f_send, f_got,
    by_send, by, bz, ey_send, ey, emf, ez, mag_new,
    load_sems, out_sems, send_sems, ids_sem, v_sem, f_sem, by_sem, bz_sems, ey_sem, ez_sems,
):
    n = cols * rows
    width = EDGE * n
    me, z = lax.axis_index("xy"), lax.axis_index("gz")
    my_x, my_y = me // rows, lax.rem(me, rows)

    def peer(j):
        return lax.rem(my_x + j // rows, cols) * rows + lax.rem(my_y + j % rows, rows)

    def slot_there(j):
        return (-(j // rows)) % cols * rows + (-(j % rows)) % rows

    above, below = lax.rem(me + 1, n), lax.rem(me + n - 1, n)
    upper, lower = lax.rem(z + 1, depth), lax.rem(z + depth - 1, depth)

    loads = [pltpu.make_async_copy(mag, field, load_sems.at[3])] + [
        pltpu.make_async_copy(vel.at[c], fine.at[c], load_sems.at[c]) for c in range(3)
    ]
    for load in loads:
        load.start()

    barrier = pltpu.get_barrier_semaphore()
    for j in range(1, n):
        pl.semaphore_signal(barrier, inc=1, device_id=(peer(j), z), device_id_type=MESH)
    for other in (upper, lower):
        pl.semaphore_signal(barrier, inc=1, device_id=(me, other), device_id_type=MESH)

    own_row = table[...]
    ids_send[...] = jnp.full((1, LANES), -1, jnp.int32)
    ids_send[:, 0:n] = own_row

    f_cell, c_cell = iota((1024, 256), 0), iota((1024, 256), 1)
    c_y = c_cell // LANES * 8 + (-(c_cell // EDGE) & 7)
    to_coarse = jnp.where(
        (f_cell // 64 == c_y) & (f_cell % 32 // 2 == c_cell % 16), 0.125, 0.0
    ).astype(jnp.bfloat16)
    j_sub = iota((n, n), 0)
    peer_row = lax.rem(my_x + j_sub // rows, cols) * rows + lax.rem(my_y + j_sub % rows, rows)
    pick = one_hot(own_row // n == peer_row).astype(jnp.bfloat16)
    pick2 = jnp.concatenate([pick, pick], axis=1)

    def means(c):
        loads[1 + c].wait()
        pair = jnp.concatenate(
            [fine[c, 0] + fine[c, 1], fine[c, 2] + fine[c, 3]], axis=0
        )
        both = dot(stacked_halves(pair), to_coarse)
        mean = both[: 2 * n] + both[2 * n :]
        by_slot = jnp.concatenate([mean[:n], mean[n:]], axis=1)
        by_peer = dot(pick2, stacked_halves(by_slot))
        for k in range(4):
            v_send[:, 4 * c + k, :] = by_peer[:, LANES * k : LANES * k + LANES]

    for c in range(3):
        means(c)

    loads[0].wait()
    for p in range(6):
        by_send[0, p : p + 1, :] = field[p // 2, p % 2, EDGE - 1 : EDGE, :]
        by_send[1, p : p + 1, :] = field[p // 2, p % 2, 0:1, :]

    pl.semaphore_wait(barrier, n + 1)

    def remote(src, dst, sent, got, xy, gz):
        return pltpu.make_async_remote_copy(
            src_ref=src, dst_ref=dst, send_sem=sent, recv_sem=got,
            device_id=(xy, gz), device_id_type=MESH,
        )

    for j in range(1, n):
        remote(ids_send, ids.at[pl.ds(slot_there(j), 1)], send_sems.at[0], ids_sem, peer(j), z).start()
    edges = [
        remote(field.at[:, 1], bz.at[0], send_sems.at[1], bz_sems.at[0], me, upper),
        remote(field.at[:, 0], bz.at[1], send_sems.at[2], bz_sems.at[1], me, lower),
        remote(by_send.at[0], by.at[0], send_sems.at[3], by_sem.at[0], above, z),
        remote(by_send.at[1], by.at[1], send_sems.at[4], by_sem.at[1], below, z),
    ]
    for edge in edges:
        edge.start()
    for j in range(1, n):
        remote(v_send.at[j], v_got.at[slot_there(j)], send_sems.at[5], v_sem, peer(j), z).start()
    v_got[0] = v_send[0]
    ids[0:1, :] = ids_send[...]

    rest = pl.ds(0, n - 1)

    def wait_all(ref, sem):
        pltpu.make_async_copy(ref.at[rest], ref.at[rest], sem).wait()

    for edge in edges:
        edge.wait_recv()
    b = [[field[c, k] for k in range(2)] for c in range(3)]

    curl_terms, spread = [], []
    for c in range(3):
        along_z = [(b[c][1], bz[0, c]), (bz[1, c], b[c][0])]
        along_y = [
            shift_y(b[c][k], by[0, 2 * c + k : 2 * c + k + 1, :], by[1, 2 * c + k : 2 * c + k + 1, :])
            for k in range(2)
        ]
        along_x = [shift_x(b[c][k]) for k in range(2)]
        curl_terms.append((along_z, along_y, along_x))
        spread.append(
            [
                (along_z[k][0] + along_z[k][1])
                + (along_y[k][0] + along_y[k][1])
                + (along_x[k][0] + along_x[k][1])
                - 6.0 * b[c][k]
                for k in range(2)
            ]
        )
    force = []
    for k in range(2):
        zs, ys, xs = (
            [central(curl_terms[c][d][k]) for c in range(3)] for d in range(3)
        )
        current = [ys[2] - zs[1], zs[0] - xs[2], xs[1] - ys[0]]
        force.append([0.1 * f for f in cross(current, [b[c][k] for c in range(3)])])
    for c in range(3):
        for k in range(2):
            mag_new[c, k] = b[c][k] + 0.05 * spread[c][k]

    wait_all(ids, ids_sem)
    listed = ids[...]
    column = jnp.where((listed >= 0) & (listed // n == me), lax.rem(listed, n), 0)
    of_peer = jnp.sum(column, axis=1, keepdims=True)
    lane = iota((n, n), 1)
    turned = lane // 8 * 8 + (-lane & 7)
    give = one_hot(of_peer == turned).astype(jnp.bfloat16)
    column_row = lax.dot_general(
        jnp.ones((n, LANES), jnp.bfloat16), column.astype(jnp.float32).astype(jnp.bfloat16),
        (((1,), (1,)), ((), ())), preferred_element_type=jnp.float32,
    )
    take = one_hot(column_row == iota((n, n), 0).astype(jnp.float32)).astype(jnp.bfloat16)
    give2 = jnp.concatenate([give, give], axis=1)
    take2 = jnp.concatenate([take, take], axis=1)

    tiles = []
    for c in range(3):
        for k in range(2):
            tiles += grid_to_blocks(force[k][c], n)
    by_peer = dot(give2, stacked_halves(jnp.concatenate(tiles, axis=1)))
    for k in range(ROWS):
        f_send[:, k, :] = by_peer[:, LANES * k : LANES * k + LANES]
    for j in range(1, n):
        remote(f_send.at[j], f_got.at[slot_there(j)], send_sems.at[6], f_sem, peer(j), z).start()
    f_got[0] = f_send[0]

    wait_all(v_got, v_sem)
    blocks = dot(
        take2,
        stacked_halves(jnp.concatenate([v_got[:, k, :] for k in range(ROWS)], axis=1)),
    )
    parts = [blocks[:, LANES * k : LANES * k + LANES] for k in range(ROWS)]
    flow = [
        [blocks_to_grid(parts[4 * c + 2 * k : 4 * c + 2 * k + 2], n) for k in range(2)]
        for c in range(3)
    ]
    for k in range(2):
        e = cross([flow[c][k] for c in range(3)], [field[c, k] for c in range(3)])
        for c in range(3):
            emf[k, c] = e[c]
        for i, c in enumerate((0, 2)):
            ey_send[0, 2 * i + k : 2 * i + k + 1, :] = e[c][EDGE - 1 : EDGE, :]
            ey_send[1, 2 * i + k : 2 * i + k + 1, :] = e[c][0:1, :]
    edges2 = [
        remote(emf.at[1, pl.ds(0, 2)], ez.at[0], send_sems.at[7], ez_sems.at[0], me, upper),
        remote(emf.at[0, pl.ds(0, 2)], ez.at[1], send_sems.at[8], ez_sems.at[1], me, lower),
        remote(ey_send.at[0], ey.at[0], send_sems.at[9], ey_sem.at[0], above, z),
        remote(ey_send.at[1], ey.at[1], send_sems.at[10], ey_sem.at[1], below, z),
    ]
    for edge in edges2:
        edge.start()
    for edge in edges2:
        edge.wait_recv()

    def dz(c, k):
        return central((emf[1, c], ez[0, c]) if k == 0 else (ez[1, c], emf[0, c]))

    def dy(c, k):
        i = 2 * (c // 2) + k
        return central(shift_y(emf[k, c], ey[0, i : i + 1, :], ey[1, i : i + 1, :]))

    def dx(c, k):
        return central(shift_x(emf[k, c]))

    for k in range(2):
        mag_new[0, k] += 0.1 * (dy(2, k) - dz(1, k))
        mag_new[1, k] += 0.1 * (dz(0, k) - dx(2, k))
        mag_new[2, k] += 0.1 * (dx(1, k) - dy(0, k))
    outs = [pltpu.make_async_copy(mag_new, mag_out, out_sems.at[3])]
    outs[0].start()

    s_sub, s_lane = iota((n, n), 0), iota((n, n), 1)
    own_diagonal = jnp.where(s_sub == s_lane, own_row // n, 0).astype(jnp.float32).astype(jnp.bfloat16)
    row_of_slot = lax.dot_general(
        own_diagonal, jnp.ones((n, n), jnp.bfloat16),
        (((1,), (1,)), ((), ())), preferred_element_type=jnp.float32,
    )
    row_at = lax.rem(my_x + s_lane // rows, cols) * rows + lax.rem(my_y + s_lane % rows, rows)
    back = one_hot(row_of_slot == row_at.astype(jnp.float32)).astype(jnp.bfloat16)
    c_cell2, f_cell2 = iota((256, 1024), 0), iota((256, 1024), 1)
    to_fine = one_hot(
        (f_cell2 // 64 == c_cell2 // 16) & (f_cell2 % 32 // 2 == c_cell2 % 16)
    ).astype(jnp.bfloat16)
    wait_all(f_got, f_sem)
    for c in range(3):
        high, low = halves(
            jnp.concatenate([f_got[:, 4 * c + k, :] for k in range(4)], axis=1)
        )
        high = dot(back, high).astype(jnp.bfloat16)
        low = dot(back, low).astype(jnp.bfloat16)
        wide = dot(
            jnp.concatenate([high[:, :256], high[:, 256:], low[:, :256], low[:, 256:]], axis=0),
            to_fine,
        )
        for k in range(2):
            gain = wide[n * k : n * k + n] + wide[2 * n + n * k : 2 * n + n * k + n]
            fine[c, 2 * k] += gain
            fine[c, 2 * k + 1] += gain
        out = pltpu.make_async_copy(fine.at[c], vel_out.at[c], out_sems.at[c])
        out.start()
        outs.append(out)

    for edge in edges + edges2:
        edge.wait_send()
    pltpu.make_async_copy(ids.at[rest], ids.at[rest], send_sems.at[0]).wait()
    wait_all(v_send, send_sems.at[5])
    wait_all(f_send, send_sems.at[6])
    for out in outs:
        out.wait()


def body(cols, rows, depth, velocity, magnetic, slot_block_table):
    n = cols * rows
    width = EDGE * n
    f32 = jnp.float32
    any_place = pl.BlockSpec(memory_space=pl.ANY)
    dma = pltpu.SemaphoreType.DMA
    return pl.pallas_call(
        functools.partial(kernel, cols, rows, depth),
        out_shape=(
            jax.ShapeDtypeStruct(velocity.shape, f32),
            jax.ShapeDtypeStruct(magnetic.shape, f32),
        ),
        in_specs=[any_place, any_place, pl.BlockSpec(memory_space=pltpu.VMEM)],
        out_specs=(any_place, any_place),
        scratch_shapes=[
            pltpu.VMEM((3, 4, n, 1024), f32),
            pltpu.VMEM((3, 2, EDGE, width), f32),
            pltpu.VMEM((1, LANES), jnp.int32),
            pltpu.VMEM((n, LANES), jnp.int32),
            pltpu.VMEM((n, ROWS, LANES), f32),
            pltpu.VMEM((n, ROWS, LANES), f32),
            pltpu.VMEM((n, ROWS, LANES), f32),
            pltpu.VMEM((n, ROWS, LANES), f32),
            pltpu.VMEM((2, 6, width), f32),
            pltpu.VMEM((2, 6, width), f32),
            pltpu.VMEM((2, 3, EDGE, width), f32),
            pltpu.VMEM((2, 4, width), f32),
            pltpu.VMEM((2, 4, width), f32),
            pltpu.VMEM((2, 3, EDGE, width), f32),
            pltpu.VMEM((2, 2, EDGE, width), f32),
            pltpu.VMEM((3, 2, EDGE, width), f32),
            dma((4,)), dma((4,)), dma((11,)), dma, dma, dma,
            dma((2,)), dma((2,)), dma((2,)), dma((2,)),
        ],
        compiler_params=pltpu.CompilerParams(
            collective_id=0, has_side_effects=True, vmem_limit_bytes=48 << 20
        ),
        name="dynamo_substep",
    )(velocity, magnetic, slot_block_table.reshape(1, n))


def solution(mesh):
    n, depth = mesh.shape["xy"], mesh.shape["gz"]
    rows = {32: 8, 8: 4}[n]
    spec = P(None, "gz", "xy", None)
    return jax.shard_map(
        functools.partial(body, n // rows, rows, depth),
        mesh=mesh,
        in_specs=(spec, spec, P("xy")),
        out_specs=(spec, spec),
        check_vma=False,
    )
```

time: 126 us -> 37.1 us (0.29)
  the two profiles are of different devices: /device:TPU:8 before, /device:TPU:16 now
where the time goes in v1:
time: 37.1 us; the launch traced here: 36.9 us
  Pallas kernels  31.4 us (85%)
  local copies, waits for them, and re-layouts  4.8 us (13%)
  between operations  0.65 us (2%)
    pallas_call x1, Pallas kernels, body(): pl.pallas_call(functools.partial(kernel, cols, rows, depth), out_shape=(j...  31.4 us
    unnamed x8, local copies, waits for them, and re-layouts  4.8 us

profile of v1, /device:TPU:16, one launch (start us, length us, event | category | flops | bytes accessed | tf_op | source)
XLA Modules:
  0.0 36.9 jit_solution(9352995842926242745)
XLA Ops:
  0.6 0.0 copy-start
  0.6 1.4 %copy-done = f32[3,4,32,1024]{3,2,1,0:T(8,128)S(1)} copy-done((f32[3,4,32,1024]{3,2,1,0:T(8,128)S(1)}, f32[3,4,32,1024]{3,2,1,0:T(8,128)}, u32[]{:S(2)}) %copy-start) | copy-done | bytes 1572888
  2.0 0.0 copy-start.1
  2.0 0.9 %copy-done.1 = f32[3,2,16,512]{3,2,1,0:T(8,128)S(1)} copy-done((f32[3,2,16,512]{3,2,1,0:T(8,128)S(1)}, f32[3,2,16,512]{3,2,1,0:T(8,128)}, u32[]{:S(2)}) %copy-start.1) | copy-done | bytes 196632
  3.0 0.0 copy-start.2
  3.0 0.7 %copy-done.2 = s32[32]{0:T(128)S(1)} copy-done((s32[32]{0:T(128)S(1)}, s32[32]{0:T(128)}, u32[]{:S(2)}) %copy-start.2) | copy-done | bytes 152
  3.6 31.4 %dynamo_substep.1 = (f32[3,4,32,1024]{3,2,1,0:T(8,128)S(1)}, f32[3,2,16,512]{3,2,1,0:T(8,128)S(1)}) custom-call(f32[3,4,32,1024]{3,2,1,0:T(8,128)S(1)} %copy-done, f32[3,2,16,512]{3,2,1,0:T(8,128)S(1)} %copy-done.1, s32[1,32]{1,0:T(1,128)S(1)} %bitcast.1), custom_call_target="tpu_custom_call" | custom-call | tf_op jit(solution)/shard_map/dynamo_substep/pallas_call | solution.py:339
  35.1 1.1 %copy.7 = f32[3,4,32,1024]{3,2,1,0:T(8,128)} copy(f32[3,4,32,1024]{3,2,1,0:T(8,128)S(1)} %get-tuple-element.4) | data formatting | bytes 3145728
  36.2 0.7 %copy.8 = f32[3,2,16,512]{3,2,1,0:T(8,128)} copy(f32[3,2,16,512]{3,2,1,0:T(8,128)S(1)} %get-tuple-element.5) | data formatting | bytes 393216
Async XLA Ops:
  0.6 1.4 %copy-start = (f32[3,4,32,1024]{3,2,1,0:T(8,128)S(1)}, f32[3,4,32,1024]{3,2,1,0:T(8,128)}, u32[]{:S(2)}) copy-start(f32[3,4,32,1024]{3,2,1,0:T(8,128)} %vel.1) | copy-start | bytes 4718596
  2.0 0.9 %copy-start.1 = (f32[3,2,16,512]{3,2,1,0:T(8,128)S(1)}, f32[3,2,16,512]{3,2,1,0:T(8,128)}, u32[]{:S(2)}) copy-start(f32[3,2,16,512]{3,2,1,0:T(8,128)} %mag.1) | copy-start | bytes 589828
  3.0 0.7 %copy-start.2 = (s32[32]{0:T(128)S(1)}, s32[32]{0:T(128)}, u32[]{:S(2)}) copy-start(s32[32]{0:T(128)} %param.5) | copy-start | bytes 388

commit v2 on v1

--- a/solution.py
+++ b/solution.py
@@ -93,10 +93,10 @@
 
 def kernel(
     cols, rows, depth,
-    vel, mag, table, vel_out, mag_out,
-    fine, field, ids_send, ids, v_send, v_got, f_send, f_got,
-    by_send, by, bz, ey_send, ey, emf, ez, mag_new,
-    load_sems, out_sems, send_sems, ids_sem, v_sem, f_sem, by_sem, bz_sems, ey_sem, ez_sems,
+    vel, mag, table, fine, mag_new,
+    field, own, v_send, v_got, f_send, f_got,
+    by_send, by, bz, ey_send, ey, emf, ez,
+    load_sems, send_sems, v_sem, f_sem, by_sem, bz_sems, ey_sem, ez_sems,
 ):
     n = cols * rows
     width = EDGE * n
@@ -112,8 +112,10 @@
     above, below = lax.rem(me + 1, n), lax.rem(me + n - 1, n)
     upper, lower = lax.rem(z + 1, depth), lax.rem(z + depth - 1, depth)
 
-    loads = [pltpu.make_async_copy(mag, field, load_sems.at[3])] + [
-        pltpu.make_async_copy(vel.at[c], fine.at[c], load_sems.at[c]) for c in range(3)
+    loads = [
+        pltpu.make_async_copy(table, own, load_sems.at[0]),
+        *(pltpu.make_async_copy(vel.at[c], fine.at[c], load_sems.at[1 + c]) for c in range(3)),
+        pltpu.make_async_copy(mag, field, load_sems.at[4]),
     ]
     for load in loads:
         load.start()
@@ -121,21 +123,21 @@
     barrier = pltpu.get_barrier_semaphore()
     for j in range(1, n):
         pl.semaphore_signal(barrier, inc=1, device_id=(peer(j), z), device_id_type=MESH)
-    for other in (upper, lower):
-        pl.semaphore_signal(barrier, inc=1, device_id=(me, other), device_id_type=MESH)
-
-    own_row = table[...]
-    ids_send[...] = jnp.full((1, LANES), -1, jnp.int32)
-    ids_send[:, 0:n] = own_row
+    pl.semaphore_signal(barrier, inc=1, device_id=(me, lower), device_id_type=MESH)
 
     f_cell, c_cell = iota((1024, 256), 0), iota((1024, 256), 1)
     c_y = c_cell // LANES * 8 + (-(c_cell // EDGE) & 7)
     to_coarse = jnp.where(
         (f_cell // 64 == c_y) & (f_cell % 32 // 2 == c_cell % 16), 0.125, 0.0
     ).astype(jnp.bfloat16)
+    loads[0].wait()
+    own_row = own[...]
     j_sub = iota((n, n), 0)
     peer_row = lax.rem(my_x + j_sub // rows, cols) * rows + lax.rem(my_y + j_sub % rows, rows)
-    pick = one_hot(own_row // n == peer_row).astype(jnp.bfloat16)
+    pick = one_hot(own_row // n == peer_row)
+    columns = jnp.sum(pick * lax.rem(own_row, n).astype(jnp.float32), axis=1, keepdims=True)
+    v_send[:, ROWS, :] = jnp.broadcast_to(columns, (n, LANES))
+    pick = pick.astype(jnp.bfloat16)
     pick2 = jnp.concatenate([pick, pick], axis=1)
 
     def means(c):
@@ -153,12 +155,12 @@
     for c in range(3):
         means(c)
 
-    loads[0].wait()
+    loads[4].wait()
     for p in range(6):
         by_send[0, p : p + 1, :] = field[p // 2, p % 2, EDGE - 1 : EDGE, :]
         by_send[1, p : p + 1, :] = field[p // 2, p % 2, 0:1, :]
 
-    pl.semaphore_wait(barrier, n + 1)
+    pl.semaphore_wait(barrier, n)
 
     def remote(src, dst, sent, got, xy, gz):
         return pltpu.make_async_remote_copy(
@@ -166,26 +168,27 @@
             device_id=(xy, gz), device_id_type=MESH,
         )
 
-    for j in range(1, n):
-        remote(ids_send, ids.at[pl.ds(slot_there(j), 1)], send_sems.at[0], ids_sem, peer(j), z).start()
+    up = remote(field.at[:, 1], bz.at[0], send_sems.at[1], bz_sems.at[0], me, upper)
+    down = remote(field.at[:, 0], bz.at[1], send_sems.at[2], bz_sems.at[1], me, lower)
     edges = [
-        remote(field.at[:, 1], bz.at[0], send_sems.at[1], bz_sems.at[0], me, upper),
-        remote(field.at[:, 0], bz.at[1], send_sems.at[2], bz_sems.at[1], me, lower),
         remote(by_send.at[0], by.at[0], send_sems.at[3], by_sem.at[0], above, z),
         remote(by_send.at[1], by.at[1], send_sems.at[4], by_sem.at[1], below, z),
     ]
+    up.start()
     for edge in edges:
         edge.start()
     for j in range(1, n):
         remote(v_send.at[j], v_got.at[slot_there(j)], send_sems.at[5], v_sem, peer(j), z).start()
     v_got[0] = v_send[0]
-    ids[0:1, :] = ids_send[...]
 
     rest = pl.ds(0, n - 1)
 
     def wait_all(ref, sem):
         pltpu.make_async_copy(ref.at[rest], ref.at[rest], sem).wait()
 
+    up.wait_recv()
+    down.start()
+    down.wait_recv()
     for edge in edges:
         edge.wait_recv()
     b = [[field[c, k] for k in range(2)] for c in range(3)]
@@ -219,33 +222,14 @@
         for k in range(2):
             mag_new[c, k] = b[c][k] + 0.05 * spread[c][k]
 
-    wait_all(ids, ids_sem)
-    listed = ids[...]
-    column = jnp.where((listed >= 0) & (listed // n == me), lax.rem(listed, n), 0)
-    of_peer = jnp.sum(column, axis=1, keepdims=True)
-    lane = iota((n, n), 1)
-    turned = lane // 8 * 8 + (-lane & 7)
-    give = one_hot(of_peer == turned).astype(jnp.bfloat16)
+    wait_all(v_got, v_sem)
+    of_peer = v_got[:, ROWS, 0:n]
     column_row = lax.dot_general(
-        jnp.ones((n, LANES), jnp.bfloat16), column.astype(jnp.float32).astype(jnp.bfloat16),
+        jnp.ones((n, n), jnp.bfloat16), (of_peer * (1.0 / n)).astype(jnp.bfloat16),
         (((1,), (1,)), ((), ())), preferred_element_type=jnp.float32,
     )
     take = one_hot(column_row == iota((n, n), 0).astype(jnp.float32)).astype(jnp.bfloat16)
-    give2 = jnp.concatenate([give, give], axis=1)
     take2 = jnp.concatenate([take, take], axis=1)
-
-    tiles = []
-    for c in range(3):
-        for k in range(2):
-            tiles += grid_to_blocks(force[k][c], n)
-    by_peer = dot(give2, stacked_halves(jnp.concatenate(tiles, axis=1)))
-    for k in range(ROWS):
-        f_send[:, k, :] = by_peer[:, LANES * k : LANES * k + LANES]
-    for j in range(1, n):
-        remote(f_send.at[j], f_got.at[slot_there(j)], send_sems.at[6], f_sem, peer(j), z).start()
-    f_got[0] = f_send[0]
-
-    wait_all(v_got, v_sem)
     blocks = dot(
         take2,
         stacked_halves(jnp.concatenate([v_got[:, k, :] for k in range(ROWS)], axis=1)),
@@ -270,25 +254,20 @@
     ]
     for edge in edges2:
         edge.start()
-    for edge in edges2:
-        edge.wait_recv()
-
-    def dz(c, k):
-        return central((emf[1, c], ez[0, c]) if k == 0 else (ez[1, c], emf[0, c]))
-
-    def dy(c, k):
-        i = 2 * (c // 2) + k
-        return central(shift_y(emf[k, c], ey[0, i : i + 1, :], ey[1, i : i + 1, :]))
-
-    def dx(c, k):
-        return central(shift_x(emf[k, c]))
-
-    for k in range(2):
-        mag_new[0, k] += 0.1 * (dy(2, k) - dz(1, k))
-        mag_new[1, k] += 0.1 * (dz(0, k) - dx(2, k))
-        mag_new[2, k] += 0.1 * (dx(1, k) - dy(0, k))
-    outs = [pltpu.make_async_copy(mag_new, mag_out, out_sems.at[3])]
-    outs[0].start()
+    lane = iota((n, n), 1)
+    turned = lane // 8 * 8 + (-lane & 7)
+    give = one_hot(of_peer == turned.astype(jnp.float32)).astype(jnp.bfloat16)
+    give2 = jnp.concatenate([give, give], axis=1)
+    tiles = []
+    for c in range(3):
+        for k in range(2):
+            tiles += grid_to_blocks(force[k][c], n)
+    by_peer = dot(give2, stacked_halves(jnp.concatenate(tiles, axis=1)))
+    for k in range(ROWS):
+        f_send[:, k, :] = by_peer[:, LANES * k : LANES * k + LANES]
+    for j in range(1, n):
+        remote(f_send.at[j], f_got.at[slot_there(j)], send_sems.at[6], f_sem, peer(j), z).start()
+    f_got[0] = f_send[0]
 
     s_sub, s_lane = iota((n, n), 0), iota((n, n), 1)
     own_diagonal = jnp.where(s_sub == s_lane, own_row // n, 0).astype(jnp.float32).astype(jnp.bfloat16)
@@ -317,40 +296,62 @@
             gain = wide[n * k : n * k + n] + wide[2 * n + n * k : 2 * n + n * k + n]
             fine[c, 2 * k] += gain
             fine[c, 2 * k + 1] += gain
-        out = pltpu.make_async_copy(fine.at[c], vel_out.at[c], out_sems.at[c])
-        out.start()
-        outs.append(out)
-
-    for edge in edges + edges2:
+
+    for edge in edges2:
+        edge.wait_recv()
+
+    def dz(c, k):
+        return central((emf[1, c], ez[0, c]) if k == 0 else (ez[1, c], emf[0, c]))
+
+    def dy(c, k):
+        i = 2 * (c // 2) + k
+        return central(shift_y(emf[k, c], ey[0, i : i + 1, :], ey[1, i : i + 1, :]))
+
+    def dx(c, k):
+        return central(shift_x(emf[k, c]))
+
+    for k in range(2):
+        mag_new[0, k] += 0.1 * (dy(2, k) - dz(1, k))
+        mag_new[1, k] += 0.1 * (dz(0, k) - dx(2, k))
+        mag_new[2, k] += 0.1 * (dx(1, k) - dy(0, k))
+
+    for edge in [up, down] + edges + edges2:
         edge.wait_send()
-    pltpu.make_async_copy(ids.at[rest], ids.at[rest], send_sems.at[0]).wait()
     wait_all(v_send, send_sems.at[5])
     wait_all(f_send, send_sems.at[6])
-    for out in outs:
-        out.wait()
+
+
+def write_out(fine, mag_new, vel_out, mag_out, sems):
+    copies = [
+        pltpu.make_async_copy(fine, vel_out, sems.at[0]),
+        pltpu.make_async_copy(mag_new, mag_out, sems.at[1]),
+    ]
+    for copy in copies:
+        copy.start()
+    for copy in copies:
+        copy.wait()
 
 
 def body(cols, rows, depth, velocity, magnetic, slot_block_table):
     n = cols * rows
     width = EDGE * n
     f32 = jnp.float32
-    any_place = pl.BlockSpec(memory_space=pl.ANY)
+    far = pl.BlockSpec(memory_space=pl.ANY)
+    near = pl.BlockSpec(memory_space=pltpu.VMEM)
     dma = pltpu.SemaphoreType.DMA
-    return pl.pallas_call(
+    fine, mag_new = pl.pallas_call(
         functools.partial(kernel, cols, rows, depth),
         out_shape=(
-            jax.ShapeDtypeStruct(velocity.shape, f32),
-            jax.ShapeDtypeStruct(magnetic.shape, f32),
+            pltpu.VMEM(velocity.shape, f32),
+            pltpu.VMEM(magnetic.shape, f32),
         ),
-        in_specs=[any_place, any_place, pl.BlockSpec(memory_space=pltpu.VMEM)],
-        out_specs=(any_place, any_place),
+        in_specs=[far, far, far],
+        out_specs=(near, near),
         scratch_shapes=[
-            pltpu.VMEM((3, 4, n, 1024), f32),
             pltpu.VMEM((3, 2, EDGE, width), f32),
-            pltpu.VMEM((1, LANES), jnp.int32),
-            pltpu.VMEM((n, LANES), jnp.int32),
-            pltpu.VMEM((n, ROWS, LANES), f32),
-            pltpu.VMEM((n, ROWS, LANES), f32),
+            pltpu.VMEM((1, n), jnp.int32),
+            pltpu.VMEM((n, ROWS + 1, LANES), f32),
+            pltpu.VMEM((n, ROWS + 1, LANES), f32),
             pltpu.VMEM((n, ROWS, LANES), f32),
             pltpu.VMEM((n, ROWS, LANES), f32),
             pltpu.VMEM((2, 6, width), f32),
@@ -360,15 +361,24 @@
             pltpu.VMEM((2, 4, width), f32),
             pltpu.VMEM((2, 3, EDGE, width), f32),
             pltpu.VMEM((2, 2, EDGE, width), f32),
-            pltpu.VMEM((3, 2, EDGE, width), f32),
-            dma((4,)), dma((4,)), dma((11,)), dma, dma, dma,
-            dma((2,)), dma((2,)), dma((2,)), dma((2,)),
+            dma((5,)), dma((11,)), dma, dma, dma((2,)), dma((2,)), dma((2,)), dma((2,)),
         ],
         compiler_params=pltpu.CompilerParams(
-            collective_id=0, has_side_effects=True, vmem_limit_bytes=48 << 20
+            collective_id=0, has_side_effects=True, vmem_limit_bytes=60 << 20
         ),
         name="dynamo_substep",
     )(velocity, magnetic, slot_block_table.reshape(1, n))
+    return pl.pallas_call(
+        write_out,
+        out_shape=(
+            jax.ShapeDtypeStruct(velocity.shape, f32),
+            jax.ShapeDtypeStruct(magnetic.shape, f32),
+        ),
+        in_specs=[near, near],
+        out_specs=(far, far),
+        scratch_shapes=[dma((2,))],
+        name="write_out",
+    )(*(pltpu.with_memory_space_constraint(a, pltpu.VMEM) for a in (fine, mag_new)))
 
 
 def solution(mesh):

time: 37.1 us -> 32.9 us (0.89)
  the two profiles are of different devices: /device:TPU:16 before, /device:TPU:8 now
where the time goes in v2:
time: 32.9 us; the launch traced here: 32.8 us
  Pallas kernels  32.1 us (98%)
  between operations  0.64 us (2%)
    pallas_call x1, Pallas kernels, body(): pl.pallas_call(functools.partial(kernel, cols, rows, depth), out_shape=(p...  30.9 us
    pallas_call x1, Pallas kernels, body(): pl.pallas_call(write_out, out_shape=(jax.ShapeDtypeStruct(velocity.shape,...  1.21 us

profile of v2, /device:TPU:8, one launch (start us, length us, event | category | flops | bytes accessed | tf_op | source)
XLA Modules:
  0.0 32.8 jit_solution(16346815487309798487)
XLA Ops:
  0.6 30.9 %dynamo_substep.1 = (f32[3,4,32,1024]{3,2,1,0:T(8,128)S(1)}, f32[3,2,16,512]{3,2,1,0:T(8,128)S(1)}) custom-call(f32[3,4,32,1024]{3,2,1,0:T(8,128)} %vel.1, f32[3,2,16,512]{3,2,1,0:T(8,128)} %mag.1, s32[1,32]{1,0:T(1,128)} %bitcast.1), custom_call_target="tpu_custom_call" | custom-call | tf_op jit(solution)/shard_map/dynamo_substep/pallas_call | solution.py:342
  31.5 1.2 %write_out.1 = (f32[3,4,32,1024]{3,2,1,0:T(8,128)}, f32[3,2,16,512]{3,2,1,0:T(8,128)}) custom-call(f32[3,4,32,1024]{3,2,1,0:T(8,128)S(1)} %get-tuple-element.4.fine, f32[3,2,16,512]{3,2,1,0:T(8,128)S(1)} %get-tuple-element.5.mag_new), custom_call_target="tpu_custom_call" | custom-call | tf_op jit(solution)/shard_map/write_out/pallas_call | solution.py:371

commit v3 on v2

v3 whole, which is shorter than its diff:
```python
import functools

import jax
import jax.numpy as jnp
from jax import lax
from jax.experimental import pallas as pl
from jax.experimental.pallas import tpu as pltpu
from jax.sharding import PartitionSpec as P

MESH = pl.DeviceIdType.MESH
LANES = 128
EDGE = 16
ROWS = 12


def halves(value):
    high = value.astype(jnp.bfloat16)
    return high, (value - high.astype(jnp.float32)).astype(jnp.bfloat16)


def stacked_halves(value):
    return jnp.concatenate(halves(value), axis=0)


def dot(a, b):
    return jnp.dot(a, b, preferred_element_type=jnp.float32)


def iota(shape, dim):
    return lax.broadcasted_iota(jnp.int32, shape, dim)


def one_hot(condition):
    return jnp.where(condition, 1.0, 0.0)


def turn_chunks(tile):
    t, m = iota((8, LANES), 0), iota((8, LANES), 1) // EDGE
    skewed = pltpu.roll(tile, 0, 1, stride=EDGE, stride_axis=0)
    picked = jnp.take_along_axis(skewed, (m + t) & 7, axis=0)
    return pltpu.roll(picked, 0, 1, stride=EDGE, stride_axis=0)


def blocks_to_grid(half_rows, n):
    return jnp.concatenate(
        [
            jnp.concatenate(
                [turn_chunks(rows[8 * g : 8 * g + 8]) for g in range(n // 8)], axis=1
            )
            for rows in half_rows
        ],
        axis=0,
    )


def grid_to_blocks(plane, n):
    return [
        jnp.concatenate(
            [
                turn_chunks(plane[8 * h : 8 * h + 8, LANES * g : LANES * g + LANES])
                for g in range(n // 8)
            ],
            axis=0,
        )
        for h in range(2)
    ]


def shift_x(plane):
    width = plane.shape[1]
    return (pltpu.roll(plane, width - 1, 1), pltpu.roll(plane, 1, 1))


def shift_y(plane, low, high):
    y = iota(plane.shape, 0)
    return (
        jnp.where(y == EDGE - 1, high, pltpu.roll(plane, EDGE - 1, 0)),
        jnp.where(y == 0, low, pltpu.roll(plane, 1, 0)),
    )


def central(pair):
    return (pair[0] - pair[1]) * 0.5


def cross(a, b):
    return [
        a[1] * b[2] - a[2] * b[1],
        a[2] * b[0] - a[0] * b[2],
        a[0] * b[1] - a[1] * b[0],
    ]


def kernel(
    cols, rows, depth,
    vel, mag, table, fine, mag_new,
    field, own, v_send, v_got, w_got, f_send, f_got,
    by_send, by, bz, ey_send, ey, emf, ez,
    load_sems, send_sems, entered, v_sem, w_sem, f_sem, by_sem, bz_sems, ey_sem, ez_sems,
):
    n = cols * rows
    me, z = lax.axis_index("xy"), lax.axis_index("gz")
    first, last = z == 0, z == depth - 1

    turn = jnp.where(first, 1, 0)

    def in_order(q):
        q = lax.rem(q + turn, n)
        y = q // cols
        return lax.rem(q, cols) * rows + jnp.where(2 * y < rows, y, 3 * rows // 2 - 1 - y)

    my_y = lax.rem(me, rows)
    order = jnp.where(2 * my_y < rows, my_y, 3 * rows // 2 - 1 - my_y) * cols + me // rows
    order = lax.rem(order + n - turn, n)

    def at_offset(j):
        return lax.rem(me // rows + j // rows, cols) * rows + lax.rem(my_y + j % rows, rows)

    above, below = lax.rem(me + 1, n), lax.rem(me + n - 1, n)
    upper, lower = lax.rem(z + 1, depth), lax.rem(z + depth - 1, depth)

    loads = [
        pltpu.make_async_copy(table, own, load_sems.at[0]),
        *(pltpu.make_async_copy(vel.at[c], fine.at[c], load_sems.at[1 + c]) for c in range(3)),
        pltpu.make_async_copy(mag, field, load_sems.at[4]),
    ]

    barrier = pltpu.get_barrier_semaphore()

    def greet(xy, gz):
        pl.semaphore_signal(barrier, inc=1, device_id=(xy, gz), device_id_type=MESH)

    @pl.loop(order + 1, n)
    def _(q):
        greet(in_order(q), z)

    @pl.when(jnp.logical_not(last))
    def _():
        greet(me, upper)

    @pl.when(first)
    def _():
        @pl.loop(0, n)
        def _(xy):
            greet(xy, lower)

    loads[4].start()
    for load in loads[:4]:
        load.start()
    greetings = order + jnp.where(first, 0, 1) + jnp.where(last, n, 0)

    @pl.when(greetings > 0)
    def _():
        pl.semaphore_wait(barrier, greetings)

    @pl.loop(0, order)
    def _(q):
        pl.semaphore_signal(
            entered.at[me], inc=1, device_id=(in_order(q), z), device_id_type=MESH
        )

    def remote(src, dst, sent, got, xy, gz):
        return pltpu.make_async_remote_copy(
            src_ref=src, dst_ref=dst, send_sem=sent, recv_sem=got,
            device_id=(xy, gz), device_id_type=MESH,
        )

    up = remote(field.at[:, 1], bz.at[0], send_sems.at[1], bz_sems.at[0], me, upper)
    down = remote(field.at[:, 0], bz.at[1], send_sems.at[2], bz_sems.at[1], me, lower)
    edges = [
        remote(by_send.at[0], by.at[0], send_sems.at[3], by_sem.at[0], above, z),
        remote(by_send.at[1], by.at[1], send_sems.at[4], by_sem.at[1], below, z),
    ]
    loads[4].wait()

    @pl.when(last)
    def _():
        up.start()

    @pl.when(jnp.logical_not(first))
    def _():
        down.start()

    f_cell, c_cell = iota((1024, 256), 0), iota((1024, 256), 1)
    c_y = c_cell // LANES * 8 + (-(c_cell // EDGE) & 7)
    to_coarse = jnp.where(
        (f_cell // 64 == c_y) & (f_cell % 32 // 2 == c_cell % 16), 0.125, 0.0
    ).astype(jnp.bfloat16)
    loads[0].wait()
    own_row = own[...]
    pick = one_hot(own_row // n == iota((n, n), 0))
    columns = jnp.sum(pick * lax.rem(own_row, n).astype(jnp.float32), axis=1, keepdims=True)
    v_send[:, ROWS, :] = jnp.broadcast_to(columns, (n, LANES))
    pick = pick.astype(jnp.bfloat16)
    pick2 = jnp.concatenate([pick, pick], axis=1)

    for c in range(3):
        loads[1 + c].wait()
        pair = jnp.concatenate(
            [fine[c, 0] + fine[c, 1], fine[c, 2] + fine[c, 3]], axis=0
        )
        both = dot(stacked_halves(pair), to_coarse)
        mean = both[: 2 * n] + both[2 * n :]
        by_slot = jnp.concatenate([mean[:n], mean[n:]], axis=1)
        by_peer = dot(pick2, stacked_halves(by_slot))
        for k in range(2):
            for h in range(2):
                at = LANES * (2 * k + h)
                v_send[:, 6 * k + 2 * c + h, :] = by_peer[:, at : at + LANES]

    def send_v(xy):
        remote(v_send.at[xy], v_got.at[me], send_sems.at[5], v_sem, xy, z).start()

    upper_rows = pl.ds(6, 6)

    @pl.when(last)
    def _():
        @pl.loop(0, n)
        def _(xy):
            remote(v_send.at[xy, upper_rows], w_got.at[me], send_sems.at[0], w_sem, xy, upper).start()

    @pl.loop(0, order)
    def _(q):
        send_v(in_order(q))

    for p in range(6):
        by_send[0, p : p + 1, :] = field[p // 2, p % 2, EDGE - 1 : EDGE, :]
        by_send[1, p : p + 1, :] = field[p // 2, p % 2, 0:1, :]
    v_got[me] = v_send[me]

    @pl.loop(order + 1, n)
    def _(q):
        xy = in_order(q)
        pl.semaphore_wait(entered.at[xy], 1)
        send_v(xy)

    for edge in edges:
        edge.start()

    @pl.when(jnp.logical_not(last))
    def _():
        down.wait_recv()
        up.start()

    def wait_all(ref, sem):
        rest = ref.at[pl.ds(0, n - 1)]
        pltpu.make_async_copy(rest, rest, sem).wait()

    wait_all(v_got, v_sem)
    of_peer = v_got[:, ROWS, 0:n]
    column_row = lax.dot_general(
        jnp.ones((n, n), jnp.bfloat16), (of_peer * (1.0 / n)).astype(jnp.bfloat16),
        (((1,), (1,)), ((), ())), preferred_element_type=jnp.float32,
    )
    take = one_hot(column_row == iota((n, n), 0).astype(jnp.float32)).astype(jnp.bfloat16)
    take2 = jnp.concatenate([take, take], axis=1)

    def on_grid(ref, planes):
        together = jnp.concatenate([ref[:, r, :] for r in range(6 * planes)], axis=1)
        blocks = dot(take2, stacked_halves(together))
        parts = [blocks[:, LANES * r : LANES * r + LANES] for r in range(6 * planes)]
        return [
            [blocks_to_grid(parts[6 * k + 2 * c : 6 * k + 2 * c + 2], n) for c in range(3)]
            for k in range(planes)
        ]

    flow = on_grid(v_got, 2)
    for k in range(2):
        e = cross(flow[k], [field[c, k] for c in range(3)])
        for c in range(3):
            emf[k, c] = e[c]
        for i, c in enumerate((0, 2)):
            ey_send[0, 2 * i + k : 2 * i + k + 1, :] = e[c][EDGE - 1 : EDGE, :]
            ey_send[1, 2 * i + k : 2 * i + k + 1, :] = e[c][0:1, :]
    up2 = remote(emf.at[1, pl.ds(0, 2)], ez.at[0], send_sems.at[7], ez_sems.at[0], me, upper)
    down2 = remote(emf.at[0, pl.ds(0, 2)], ez.at[1], send_sems.at[8], ez_sems.at[1], me, lower)
    edges2 = [
        remote(ey_send.at[0], ey.at[0], send_sems.at[9], ey_sem.at[0], above, z),
        remote(ey_send.at[1], ey.at[1], send_sems.at[10], ey_sem.at[1], below, z),
    ]

    @pl.when(jnp.logical_not(last))
    def _():
        up2.start()

    @pl.when(jnp.logical_not(first))
    def _():
        down2.start()

    for edge in edges2:
        edge.start()

    up.wait_recv()

    @pl.when(first)
    def _():
        down.start()
        down2.start()

    @pl.when(last)
    def _():
        down.wait_recv()

    for edge in edges:
        edge.wait_recv()

    b = [[field[c, k] for k in range(2)] for c in range(3)]
    pairs, spread = [], []
    for c in range(3):
        along_z = [(b[c][1], bz[0, c]), (bz[1, c], b[c][0])]
        along_y = [
            shift_y(b[c][k], by[0, 2 * c + k : 2 * c + k + 1, :], by[1, 2 * c + k : 2 * c + k + 1, :])
            for k in range(2)
        ]
        along_x = [shift_x(b[c][k]) for k in range(2)]
        pairs.append((along_z, along_y, along_x))
        spread.append(
            [
                (along_z[k][0] + along_z[k][1])
                + (along_y[k][0] + along_y[k][1])
                + (along_x[k][0] + along_x[k][1])
                - 6.0 * b[c][k]
                for k in range(2)
            ]
        )
    force = []
    for k in range(2):
        zs, ys, xs = ([central(pairs[c][d][k]) for c in range(3)] for d in range(3))
        current = [ys[2] - zs[1], zs[0] - xs[2], xs[1] - ys[0]]
        force.append([0.1 * f for f in cross(current, [b[c][k] for c in range(3)])])

    lane = iota((n, n), 1)
    turned = lane // 8 * 8 + (-lane & 7)
    give = one_hot(of_peer == turned.astype(jnp.float32)).astype(jnp.bfloat16)
    give2 = jnp.concatenate([give, give], axis=1)
    tiles = []
    for c in range(3):
        for k in range(2):
            tiles += grid_to_blocks(force[k][c], n)
    by_peer = dot(give2, stacked_halves(jnp.concatenate(tiles, axis=1)))
    for r in range(ROWS):
        f_send[:, r, :] = by_peer[:, LANES * r : LANES * r + LANES]

    def hops(j):
        return min(j // rows, cols - j // rows) + min(j % rows, rows - j % rows)

    for j in sorted(range(1, n), key=hops, reverse=True):
        xy = at_offset(j)
        remote(f_send.at[xy], f_got.at[me], send_sems.at[6], f_sem, xy, z).start()
    f_got[me] = f_send[me]
    for c in range(3):
        for k in range(2):
            mag_new[c, k] = b[c][k] + 0.05 * spread[c][k]

    s_sub, s_lane = iota((n, n), 0), iota((n, n), 1)
    own_diagonal = jnp.where(s_sub == s_lane, own_row // n, 0).astype(jnp.float32).astype(jnp.bfloat16)
    row_of_slot = lax.dot_general(
        own_diagonal, jnp.ones((n, n), jnp.bfloat16),
        (((1,), (1,)), ((), ())), preferred_element_type=jnp.float32,
    )
    back = one_hot(row_of_slot == s_lane.astype(jnp.float32)).astype(jnp.bfloat16)
    c_cell2, f_cell2 = iota((256, 1024), 0), iota((256, 1024), 1)
    to_fine = one_hot(
        (f_cell2 // 64 == c_cell2 // 16) & (f_cell2 % 32 // 2 == c_cell2 % 16)
    ).astype(jnp.bfloat16)

    def update():
        wait_all(f_got, f_sem)
        for c in range(3):
            high, low = halves(
                jnp.concatenate([f_got[:, 4 * c + r, :] for r in range(4)], axis=1)
            )
            high = dot(back, high).astype(jnp.bfloat16)
            low = dot(back, low).astype(jnp.bfloat16)
            wide = dot(
                jnp.concatenate([high[:, :256], high[:, 256:], low[:, :256], low[:, 256:]], axis=0),
                to_fine,
            )
            for k in range(2):
                gain = wide[n * k : n * k + n] + wide[2 * n + n * k : 2 * n + n * k + n]
                fine[c, 2 * k] += gain
                fine[c, 2 * k + 1] += gain

    def finish():
        @pl.when(jnp.logical_not(first))
        def _():
            up2.wait_recv()

        @pl.when(first)
        def _():
            every = w_got.at[:]
            pltpu.make_async_copy(every, every, w_sem).wait()
            [below_flow] = on_grid(w_got, 1)
            e = cross(below_flow, [bz[0, c] for c in range(3)])
            for c in range(2):
                ez[0, c] = e[c]

        down2.wait_recv()
        for edge in edges2:
            edge.wait_recv()

        def dz(c, k):
            return central((emf[1, c], ez[0, c]) if k == 0 else (ez[1, c], emf[0, c]))

        def dy(c, k):
            i = 2 * (c // 2) + k
            return central(shift_y(emf[k, c], ey[0, i : i + 1, :], ey[1, i : i + 1, :]))

        def dx(c, k):
            return central(shift_x(emf[k, c]))

        for k in range(2):
            mag_new[0, k] += 0.1 * (dy(2, k) - dz(1, k))
            mag_new[1, k] += 0.1 * (dz(0, k) - dx(2, k))
            mag_new[2, k] += 0.1 * (dx(1, k) - dy(0, k))

    update()
    finish()

    for edge in [up, down, down2, *edges, *edges2]:
        edge.wait_send()

    @pl.when(jnp.logical_not(last))
    def _():
        up2.wait_send()

    @pl.when(last)
    def _():
        every = w_got.at[:]
        pltpu.make_async_copy(every, every, send_sems.at[0]).wait()

    wait_all(v_send, send_sems.at[5])
    wait_all(f_send, send_sems.at[6])


def write_out(fine, mag_new, vel_out, mag_out, sems):
    copies = [
        pltpu.make_async_copy(fine, vel_out, sems.at[0]),
        pltpu.make_async_copy(mag_new, mag_out, sems.at[1]),
    ]
    for copy in copies:
        copy.start()
    for copy in copies:
        copy.wait()


def body(cols, rows, depth, velocity, magnetic, slot_block_table):
    n = cols * rows
    width = EDGE * n
    f32 = jnp.float32
    far = pl.BlockSpec(memory_space=pl.ANY)
    near = pl.BlockSpec(memory_space=pltpu.VMEM)
    dma = pltpu.SemaphoreType.DMA
    fine, mag_new = pl.pallas_call(
        functools.partial(kernel, cols, rows, depth),
        out_shape=(
            pltpu.VMEM(velocity.shape, f32),
            pltpu.VMEM(magnetic.shape, f32),
        ),
        in_specs=[far, far, far],
        out_specs=(near, near),
        scratch_shapes=[
            pltpu.VMEM((3, 2, EDGE, width), f32),
            pltpu.VMEM((1, n), jnp.int32),
            pltpu.VMEM((n, ROWS + 1, LANES), f32),
            pltpu.VMEM((n, ROWS + 1, LANES), f32),
            pltpu.VMEM((n, 6, LANES), f32),
            pltpu.VMEM((n, ROWS, LANES), f32),
            pltpu.VMEM((n, ROWS, LANES), f32),
            pltpu.VMEM((2, 6, width), f32),
            pltpu.VMEM((2, 6, width), f32),
            pltpu.VMEM((2, 3, EDGE, width), f32),
            pltpu.VMEM((2, 4, width), f32),
            pltpu.VMEM((2, 4, width), f32),
            pltpu.VMEM((2, 3, EDGE, width), f32),
            pltpu.VMEM((2, 2, EDGE, width), f32),
            dma((5,)), dma((11,)), pltpu.SemaphoreType.REGULAR((n,)), dma, dma, dma, dma((2,)), dma((2,)), dma((2,)), dma((2,)),
        ],
        compiler_params=pltpu.CompilerParams(
            collective_id=0, has_side_effects=True, vmem_limit_bytes=60 << 20
        ),
        name="dynamo_substep",
    )(velocity, magnetic, slot_block_table.reshape(1, n))
    return pl.pallas_call(
        write_out,
        out_shape=(
            jax.ShapeDtypeStruct(velocity.shape, f32),
            jax.ShapeDtypeStruct(magnetic.shape, f32),
        ),
        in_specs=[near, near],
        out_specs=(far, far),
        scratch_shapes=[dma((2,))],
        name="write_out",
    )(*(pltpu.with_memory_space_constraint(a, pltpu.VMEM) for a in (fine, mag_new)))


def solution(mesh):
    n, depth = mesh.shape["xy"], mesh.shape["gz"]
    rows = {32: 8, 8: 4}[n]
    spec = P(None, "gz", "xy", None)
    return jax.shard_map(
        functools.partial(body, n // rows, rows, depth),
        mesh=mesh,
        in_specs=(spec, spec, P("xy")),
        out_specs=(spec, spec),
        check_vma=False,
    )
```

time: 32.9 us -> 32.1 us (0.976)
  the two profiles are of different devices: /device:TPU:8 before, /device:TPU:2 now
where the time goes in v3:
time: 32.1 us; the launch traced here: 31.9 us
  Pallas kernels  31.3 us (98%)
  between operations  0.64 us (2%)
    pallas_call x1, Pallas kernels, body(): pl.pallas_call(functools.partial(kernel, cols, rows, depth), out_shape=(p...  30.1 us
    pallas_call x1, Pallas kernels, body(): pl.pallas_call(write_out, out_shape=(jax.ShapeDtypeStruct(velocity.shape,...  1.21 us

profile of v3, /device:TPU:2, one launch (start us, length us, event | category | flops | bytes accessed | tf_op | source)
XLA Modules:
  0.0 31.9 jit_solution(15876695270430695465)
XLA Ops:
  0.6 30.1 %dynamo_substep.1 = (f32[3,4,32,1024]{3,2,1,0:T(8,128)S(1)}, f32[3,2,16,512]{3,2,1,0:T(8,128)S(1)}) custom-call(f32[3,4,32,1024]{3,2,1,0:T(8,128)} %vel.1, f32[3,2,16,512]{3,2,1,0:T(8,128)} %mag.1, s32[1,32]{1,0:T(1,128)} %bitcast.1), custom_call_target="tpu_custom_call" | custom-call | tf_op jit(solution)/shard_map/dynamo_substep/pallas_call | solution.py:454
  30.7 1.2 %write_out.1 = (f32[3,4,32,1024]{3,2,1,0:T(8,128)}, f32[3,2,16,512]{3,2,1,0:T(8,128)}) custom-call(f32[3,4,32,1024]{3,2,1,0:T(8,128)S(1)} %get-tuple-element.4.fine, f32[3,2,16,512]{3,2,1,0:T(8,128)S(1)} %get-tuple-element.5.mag_new), custom_call_target="tpu_custom_call" | custom-call | tf_op jit(solution)/shard_map/write_out/pallas_call | solution.py:484

commit v4 on v3

v4 whole, which is shorter than its diff:
```python
import functools

import jax
import jax.numpy as jnp
from jax import lax
from jax.experimental import pallas as pl
from jax.experimental.pallas import tpu as pltpu
from jax.sharding import PartitionSpec as P

MESH = pl.DeviceIdType.MESH
LANES = 128
EDGE = 16
ROWS = 12
HALF_ROWS = 6


def halves(value):
    high = value.astype(jnp.bfloat16)
    return high, (value - high.astype(jnp.float32)).astype(jnp.bfloat16)


def stacked_halves(value):
    return jnp.concatenate(halves(value), axis=0)


def dot(a, b):
    return jnp.dot(a, b, preferred_element_type=jnp.float32)


def iota(shape, dim):
    return lax.broadcasted_iota(jnp.int32, shape, dim)


def one_hot(condition):
    return jnp.where(condition, 1.0, 0.0)


def turn_chunks(tile):
    t, m = iota((8, LANES), 0), iota((8, LANES), 1) // EDGE
    skewed = pltpu.roll(tile, 0, 1, stride=EDGE, stride_axis=0)
    picked = jnp.take_along_axis(skewed, (m + t) & 7, axis=0)
    return pltpu.roll(picked, 0, 1, stride=EDGE, stride_axis=0)


def blocks_to_grid(half_rows, n):
    return jnp.concatenate(
        [
            jnp.concatenate(
                [turn_chunks(rows[8 * g : 8 * g + 8]) for g in range(n // 8)], axis=1
            )
            for rows in half_rows
        ],
        axis=0,
    )


def grid_to_blocks(plane, n):
    return [
        jnp.concatenate(
            [
                turn_chunks(plane[8 * h : 8 * h + 8, LANES * g : LANES * g + LANES])
                for g in range(n // 8)
            ],
            axis=0,
        )
        for h in range(2)
    ]


def shift_x(plane):
    width = plane.shape[1]
    return (pltpu.roll(plane, width - 1, 1), pltpu.roll(plane, 1, 1))


def shift_y(plane, low, high):
    y = iota(plane.shape, 0)
    return (
        jnp.where(y == EDGE - 1, high, pltpu.roll(plane, EDGE - 1, 0)),
        jnp.where(y == 0, low, pltpu.roll(plane, 1, 0)),
    )


def central(pair):
    return (pair[0] - pair[1]) * 0.5


def cross(a, b):
    return [
        a[1] * b[2] - a[2] * b[1],
        a[2] * b[0] - a[0] * b[2],
        a[0] * b[1] - a[1] * b[0],
    ]


def kernel(
    cols, rows, depth,
    vel, mag, table, fine, mag_new,
    field, own, ids_send, ids, v_send, v_got, w_got, f_send, f_got,
    by_send, by, bz, ey_send, ey, emf, ez,
    load_sems, send_sems, entered, ids_sem, v_sem, w_sem, f_sem, by_sem, bz_sems, ey_sem, ez_sems,
):
    n = cols * rows
    me, z = lax.axis_index("xy"), lax.axis_index("gz")
    first, last = z == 0, z == depth - 1

    def at_offset(j):
        return ((me // rows + j // rows) & (cols - 1)) * rows + ((me + j) & (rows - 1))

    def hops(j):
        return min(j // rows, cols - j // rows) + min(j % rows, rows - j % rows)

    def order_of(xy):
        y = xy & (rows - 1)
        return jnp.where(2 * y < rows, y, 3 * rows // 2 - 1 - y) * cols + xy // rows

    def rank(xy):
        return jnp.where(first, jnp.where(xy == 0, 1, 0), jnp.where(last, order_of(xy), 0))

    my_rank = rank(me)
    farthest_first = sorted(range(1, n), key=hops, reverse=True)
    peers = [(xy, rank(xy)) for xy in map(at_offset, farthest_first)]
    alike = jnp.where(first, n - 2 + my_rank, jnp.where(last, my_rank, n - 1))

    def each_ready(act):
        for xy, its_rank in peers:
            pl.when(its_rank <= my_rank)(functools.partial(act, xy))

    def each_later(act):
        for xy, its_rank in peers:
            pl.when(its_rank > my_rank)(functools.partial(act, xy))

    above, below = lax.rem(me + 1, n), lax.rem(me + n - 1, n)
    upper, lower = lax.rem(z + 1, depth), lax.rem(z + depth - 1, depth)

    loads = [
        pltpu.make_async_copy(table, own, load_sems.at[0]),
        *(pltpu.make_async_copy(vel.at[c], fine.at[c], load_sems.at[1 + c]) for c in range(3)),
        pltpu.make_async_copy(mag, field, load_sems.at[4]),
    ]

    barrier = pltpu.get_barrier_semaphore()

    def greet(xy, gz):
        pl.semaphore_signal(barrier, inc=1, device_id=(xy, gz), device_id_type=MESH)

    for xy, its_rank in peers:
        pl.when(its_rank >= my_rank)(functools.partial(greet, xy, z))

    @pl.when(jnp.logical_not(last))
    def _():
        greet(me, upper)

    @pl.when(first)
    def _():
        for xy in range(n):
            greet(xy, lower)

    loads[4].start()
    for load in loads[:4]:
        load.start()
    greetings = alike + jnp.where(first, 0, 1) + jnp.where(last, n, 0)

    @pl.when(greetings > 0)
    def _():
        pl.semaphore_wait(barrier, greetings)

    def say_entered(xy):
        pl.semaphore_signal(entered.at[me], inc=1, device_id=(xy, z), device_id_type=MESH)

    @pl.when(my_rank > 0)
    def _():
        for xy, its_rank in peers:
            pl.when(its_rank < my_rank)(functools.partial(say_entered, xy))

    def remote(src, dst, sent, got, xy, gz):
        return pltpu.make_async_remote_copy(
            src_ref=src, dst_ref=dst, send_sem=sent, recv_sem=got,
            device_id=(xy, gz), device_id_type=MESH,
        )

    up_xy = remote(
        mag.at[pl.ds(0, 2), 1], bz.at[0, pl.ds(0, 2)], send_sems.at[1], bz_sems.at[0], me, upper
    )
    up_z = remote(mag.at[2, 1], bz.at[0, 2], send_sems.at[13], bz_sems.at[2], me, upper)
    down = remote(mag.at[:, 0], bz.at[1], send_sems.at[2], bz_sems.at[1], me, lower)
    edges = [
        remote(by_send.at[0], by.at[0], send_sems.at[3], by_sem.at[0], above, z),
        remote(by_send.at[1], by.at[1], send_sems.at[4], by_sem.at[1], below, z),
    ]

    @pl.when(last)
    def _():
        up_xy.start()
        up_z.start()

    @pl.when(jnp.logical_not(first))
    def _():
        down.start()

    f_cell, c_cell = iota((1024, 256), 0), iota((1024, 256), 1)
    c_y = c_cell // LANES * 8 + (-(c_cell // EDGE) & 7)
    to_coarse = jnp.where(
        (f_cell // 64 == c_y) & (f_cell % 32 // 2 == c_cell % 16), 0.125, 0.0
    ).astype(jnp.bfloat16)
    loads[0].wait()
    own_row = own[...]
    ids_send[...] = jnp.full((1, LANES), -1, jnp.int32)
    ids_send[:, 0:n] = own_row
    ids[pl.ds(me, 1), :] = ids_send[...]

    def send_ids(xy):
        there = ids.at[pl.ds(me, 1)]
        remote(ids_send, there, send_sems.at[11], ids_sem, xy, z).start()

    each_ready(send_ids)

    pick = one_hot(own_row // n == iota((n, n), 0))
    pick = pick.astype(jnp.bfloat16)
    pick2 = jnp.concatenate([pick, pick], axis=1)

    for c in range(3):
        loads[1 + c].wait()
        pair = jnp.concatenate(
            [fine[c, 0] + fine[c, 1], fine[c, 2] + fine[c, 3]], axis=0
        )
        both = dot(stacked_halves(pair), to_coarse)
        mean = both[: 2 * n] + both[2 * n :]
        by_slot = jnp.concatenate([mean[:n], mean[n:]], axis=1)
        by_peer = dot(pick2, stacked_halves(by_slot))
        for k in range(2):
            for h in range(2):
                at = LANES * (2 * k + h)
                v_send[:, 6 * k + 2 * c + h, :] = by_peer[:, at : at + LANES]

    def send_v(xy):
        remote(v_send.at[xy], v_got.at[me], send_sems.at[12], v_sem, xy, z).start()

    upper_rows = pl.ds(6, 6)

    @pl.when(last)
    def _():
        for xy in range(n):
            remote(v_send.at[xy, upper_rows], w_got.at[me], send_sems.at[0], w_sem, xy, upper).start()

    each_ready(send_v)

    loads[4].wait()
    for p in range(6):
        by_send[0, p : p + 1, :] = field[p // 2, p % 2, EDGE - 1 : EDGE, :]
        by_send[1, p : p + 1, :] = field[p // 2, p % 2, 0:1, :]
    v_got[me] = v_send[me]

    @pl.when(jnp.logical_or(first, last))
    def _():
        @each_later
        def _(xy):
            pl.semaphore_wait(entered.at[xy], 1)
            send_ids(xy)
            send_v(xy)

    for edge in edges:
        edge.start()

    @pl.when(jnp.logical_not(last))
    def _():
        down.wait_recv()
        up_xy.start()
        up_z.start()

    def wait_all(ref, sem):
        rest = ref.at[pl.ds(0, n - 1)]
        pltpu.make_async_copy(rest, rest, sem).wait()

    wait_all(ids, ids_sem)
    listed = ids[...]
    column = jnp.where((listed >= 0) & (listed // n == me), lax.rem(listed, n), 0).astype(jnp.float32)
    of_peer = jnp.sum(column, axis=1, keepdims=True)
    lane = iota((n, n), 1)
    turned = lane // 8 * 8 + (-lane & 7)
    give = one_hot(of_peer == turned.astype(jnp.float32)).astype(jnp.bfloat16)
    give2 = jnp.concatenate([give, give], axis=1)
    column_row = lax.dot_general(
        jnp.ones((n, LANES), jnp.bfloat16), column.astype(jnp.bfloat16),
        (((1,), (1,)), ((), ())), preferred_element_type=jnp.float32,
    )
    take = one_hot(column_row == iota((n, n), 0).astype(jnp.float32)).astype(jnp.bfloat16)
    take2 = jnp.concatenate([take, take], axis=1)

    def on_grid(ref, planes):
        together = jnp.concatenate([ref[:, r, :] for r in range(6 * planes)], axis=1)
        blocks = dot(take2, stacked_halves(together))
        parts = [blocks[:, LANES * r : LANES * r + LANES] for r in range(6 * planes)]
        return [
            [blocks_to_grid(parts[6 * k + 2 * c : 6 * k + 2 * c + 2], n) for c in range(3)]
            for k in range(planes)
        ]

    up2 = remote(emf.at[1, pl.ds(0, 2)], ez.at[0], send_sems.at[7], ez_sems.at[0], me, upper)
    down2 = remote(emf.at[0, pl.ds(0, 2)], ez.at[1], send_sems.at[8], ez_sems.at[1], me, lower)
    edges2 = [
        remote(ey_send.at[0], ey.at[0], send_sems.at[9], ey_sem.at[0], above, z),
        remote(ey_send.at[1], ey.at[1], send_sems.at[10], ey_sem.at[1], below, z),
    ]

    def make_emf():
        wait_all(v_got, v_sem)
        flow = on_grid(v_got, 2)
        for k in range(2):
            e = cross(flow[k], [field[c, k] for c in range(3)])
            for c in range(3):
                emf[k, c] = e[c]
            for i, c in enumerate((0, 2)):
                ey_send[0, 2 * i + k : 2 * i + k + 1, :] = e[c][EDGE - 1 : EDGE, :]
                ey_send[1, 2 * i + k : 2 * i + k + 1, :] = e[c][0:1, :]

        @pl.when(jnp.logical_not(last))
        def _():
            up2.start()

        for edge in edges2:
            edge.start()

    @pl.when(first)
    def _():
        make_emf()

    for edge in edges:
        edge.wait_recv()

    @pl.when(last)
    def _():
        down.wait_recv()

    def make_force(k):
        b = [field[c, k] for c in range(3)]
        along_x = [shift_x(b[c]) for c in range(3)]
        along_y = [
            shift_y(b[c], by[0, 2 * c + k : 2 * c + k + 1, :], by[1, 2 * c + k : 2 * c + k + 1, :])
            for c in range(3)
        ]

        def along_z(c):
            return (bz[1, c], field[c, 0]) if k else (field[c, 1], bz[0, c])

        dx, dy = ([central(pair) for pair in pairs] for pairs in (along_x, along_y))
        dz = [central(along_z(c)) for c in range(2)]
        current = [dy[2] - dz[1], dz[0] - dx[2], dx[1] - dy[0]]
        tiles = [tile for f in cross(current, b) for tile in grid_to_blocks(0.1 * f, n)]
        by_peer = dot(give2, stacked_halves(jnp.concatenate(tiles, axis=1)))
        for r in range(HALF_ROWS):
            f_send[k, :, r, :] = by_peer[:, LANES * r : LANES * r + LANES]
        for xy, _ in peers:
            remote(f_send.at[k, xy], f_got.at[k, me], send_sems.at[5 + k], f_sem.at[k], xy, z).start()
        f_got[k, me] = f_send[k, me]
        if not k:
            up_z.wait_recv()
        for c in range(3):
            z_pair = along_z(c)
            lap = (
                (z_pair[0] + z_pair[1])
                + (along_y[c][0] + along_y[c][1])
                + (along_x[c][0] + along_x[c][1])
                - 6.0 * b[c]
            )
            mag_new[c, k] = b[c] + 0.05 * lap

    make_force(1)
    up_xy.wait_recv()

    @pl.when(first)
    def _():
        down.start()

    make_force(0)

    @pl.when(jnp.logical_not(first))
    def _():
        make_emf()

    down2.start()

    s_sub, s_lane = iota((n, n), 0), iota((n, n), 1)
    own_diagonal = jnp.where(s_sub == s_lane, own_row // n, 0).astype(jnp.float32).astype(jnp.bfloat16)
    row_of_slot = lax.dot_general(
        own_diagonal, jnp.ones((n, n), jnp.bfloat16),
        (((1,), (1,)), ((), ())), preferred_element_type=jnp.float32,
    )
    back = one_hot(row_of_slot == s_lane.astype(jnp.float32)).astype(jnp.bfloat16)
    c_cell2, f_cell2 = iota((256, 1024), 0), iota((256, 1024), 1)
    to_fine = one_hot(
        (f_cell2 // 64 == c_cell2 // 16) & (f_cell2 % 32 // 2 == c_cell2 % 16)
    ).astype(jnp.bfloat16)

    def update(k):
        wait_all(f_got.at[k], f_sem.at[k])
        high, low = halves(jnp.concatenate([f_got[k, :, r, :] for r in range(HALF_ROWS)], axis=1))
        parts = [dot(back, part).astype(jnp.bfloat16) for part in (high, low)]
        wide = dot(
            jnp.concatenate([part[:, 256 * c : 256 * c + 256] for part in parts for c in range(3)], axis=0),
            to_fine,
        )
        for c in range(3):
            gain = wide[n * c : n * c + n] + wide[n * (3 + c) : n * (4 + c)]
            fine[c, 2 * k] += gain
            fine[c, 2 * k + 1] += gain

    def finish():
        @pl.when(jnp.logical_not(first))
        def _():
            up2.wait_recv()

        @pl.when(first)
        def _():
            every = w_got.at[:]
            pltpu.make_async_copy(every, every, w_sem).wait()
            [below_flow] = on_grid(w_got, 1)
            e = cross(below_flow, [bz[0, c] for c in range(3)])
            for c in range(2):
                ez[0, c] = e[c]

        down2.wait_recv()
        for edge in edges2:
            edge.wait_recv()

        def dz(c, k):
            return central((emf[1, c], ez[0, c]) if k == 0 else (ez[1, c], emf[0, c]))

        def dy(c, k):
            i = 2 * (c // 2) + k
            return central(shift_y(emf[k, c], ey[0, i : i + 1, :], ey[1, i : i + 1, :]))

        def dx(c, k):
            return central(shift_x(emf[k, c]))

        for k in range(2):
            mag_new[0, k] += 0.1 * (dy(2, k) - dz(1, k))
            mag_new[1, k] += 0.1 * (dz(0, k) - dx(2, k))
            mag_new[2, k] += 0.1 * (dx(1, k) - dy(0, k))

    update(1)
    finish()
    update(0)

    for edge in [up_xy, up_z, down, down2, *edges, *edges2]:
        edge.wait_send()

    @pl.when(jnp.logical_not(last))
    def _():
        up2.wait_send()

    @pl.when(last)
    def _():
        every = w_got.at[:]
        pltpu.make_async_copy(every, every, send_sems.at[0]).wait()

    wait_all(ids, send_sems.at[11])
    wait_all(v_send, send_sems.at[12])
    for k in range(2):
        wait_all(f_send.at[k], send_sems.at[5 + k])


def write_out(fine, mag_new, vel_out, mag_out, sems):
    copies = [
        pltpu.make_async_copy(fine.at[c, pl.ds(2 * k, 2)], vel_out.at[c, pl.ds(2 * k, 2)], sems.at[2 * c + k])
        for c in range(3)
        for k in range(2)
    ]
    copies += [pltpu.make_async_copy(mag_new, mag_out, sems.at[6])]
    for copy in copies:
        copy.start()
    for copy in copies:
        copy.wait()


def body(cols, rows, depth, velocity, magnetic, slot_block_table):
    n = cols * rows
    width = EDGE * n
    f32 = jnp.float32
    far = pl.BlockSpec(memory_space=pl.ANY)
    near = pl.BlockSpec(memory_space=pltpu.VMEM)
    dma = pltpu.SemaphoreType.DMA
    fine, mag_new = pl.pallas_call(
        functools.partial(kernel, cols, rows, depth),
        out_shape=(
            pltpu.VMEM(velocity.shape, f32),
            pltpu.VMEM(magnetic.shape, f32),
        ),
        in_specs=[far, far, far],
        out_specs=(near, near),
        scratch_shapes=[
            pltpu.VMEM((3, 2, EDGE, width), f32),
            pltpu.VMEM((1, n), jnp.int32),
            pltpu.VMEM((1, LANES), jnp.int32),
            pltpu.VMEM((n, LANES), jnp.int32),
            pltpu.VMEM((n, ROWS, LANES), f32),
            pltpu.VMEM((n, ROWS, LANES), f32),
            pltpu.VMEM((n, 6, LANES), f32),
            pltpu.VMEM((2, n, HALF_ROWS, LANES), f32),
            pltpu.VMEM((2, n, HALF_ROWS, LANES), f32),
            pltpu.VMEM((2, 6, width), f32),
            pltpu.VMEM((2, 6, width), f32),
            pltpu.VMEM((2, 3, EDGE, width), f32),
            pltpu.VMEM((2, 4, width), f32),
            pltpu.VMEM((2, 4, width), f32),
            pltpu.VMEM((2, 3, EDGE, width), f32),
            pltpu.VMEM((2, 2, EDGE, width), f32),
            dma((5,)), dma((14,)), pltpu.SemaphoreType.REGULAR((n,)), dma, dma, dma, dma((2,)), dma((2,)), dma((3,)), dma((2,)), dma((2,)),
        ],
        compiler_params=pltpu.CompilerParams(
            collective_id=0, has_side_effects=True, vmem_limit_bytes=60 << 20
        ),
        name="dynamo_substep",
    )(velocity, magnetic, slot_block_table.reshape(1, n))
    return pl.pallas_call(
        write_out,
        out_shape=(
            jax.ShapeDtypeStruct(velocity.shape, f32),
            jax.ShapeDtypeStruct(magnetic.shape, f32),
        ),
        in_specs=[near, near],
        out_specs=(far, far),
        scratch_shapes=[dma((7,))],
        name="write_out",
    )(*(pltpu.with_memory_space_constraint(a, pltpu.VMEM) for a in (fine, mag_new)))


def solution(mesh):
    n, depth = mesh.shape["xy"], mesh.shape["gz"]
    rows = {32: 8, 8: 4}[n]
    spec = P(None, "gz", "xy", None)
    return jax.shard_map(
        functools.partial(body, n // rows, rows, depth),
        mesh=mesh,
        in_specs=(spec, spec, P("xy")),
        out_specs=(spec, spec),
        check_vma=False,
    )
```

time: 32.1 us -> 30.1 us (0.938)
  the two profiles are of different devices: /device:TPU:2 before, /device:TPU:8 now
where the time goes in v4:
time: 30.1 us; the launch traced here: 30 us
  Pallas kernels  29.3 us (97%)
  between operations  0.64 us (2%)
    pallas_call x1, Pallas kernels, body(): pl.pallas_call(functools.partial(kernel, cols, rows, depth), out_shape=(p...  28.1 us
    pallas_call x1, Pallas kernels, body(): pl.pallas_call(write_out, out_shape=(jax.ShapeDtypeStruct(velocity.shape,...  1.26 us

profile of v4, /device:TPU:8, one launch (start us, length us, event | category | flops | bytes accessed | tf_op | source)
XLA Modules:
  0.0 30.0 jit_solution(6791304252071742758)
XLA Ops:
  0.6 28.1 %dynamo_substep.1 = (f32[3,4,32,1024]{3,2,1,0:T(8,128)S(1)}, f32[3,2,16,512]{3,2,1,0:T(8,128)S(1)}) custom-call(f32[3,4,32,1024]{3,2,1,0:T(8,128)} %vel.1, f32[3,2,16,512]{3,2,1,0:T(8,128)} %mag.1, s32[1,32]{1,0:T(1,128)} %bitcast.1), custom_call_target="tpu_custom_call" | custom-call | tf_op jit(solution)/shard_map/dynamo_substep/pallas_call | solution.py:482
  28.7 1.3 %write_out.1 = (f32[3,4,32,1024]{3,2,1,0:T(8,128)}, f32[3,2,16,512]{3,2,1,0:T(8,128)}) custom-call(f32[3,4,32,1024]{3,2,1,0:T(8,128)S(1)} %get-tuple-element.4.fine, f32[3,2,16,512]{3,2,1,0:T(8,128)S(1)} %get-tuple-element.5.mag_new), custom_call_target="tpu_custom_call" | custom-call | tf_op jit(solution)/shard_map/write_out/pallas_call | solution.py:514

commit v5 on v4

--- a/solution.py
+++ b/solution.py
@@ -143,8 +143,16 @@
     def greet(xy, gz):
         pl.semaphore_signal(barrier, inc=1, device_id=(xy, gz), device_id_type=MESH)
 
-    for xy, its_rank in peers:
-        pl.when(its_rank >= my_rank)(functools.partial(greet, xy, z))
+    @pl.when(last)
+    def _():
+        places = [x * rows + y for y in (*range(rows // 2), *range(rows - 1, rows // 2 - 1, -1)) for x in range(cols)]
+        for q in range(1, n):
+            pl.when(q > my_rank)(functools.partial(greet, places[q], z))
+
+    @pl.when(jnp.logical_not(jnp.logical_or(last, my_rank > 0)))
+    def _():
+        for j in farthest_first:
+            greet(at_offset(j), z)
 
     @pl.when(jnp.logical_not(last))
     def _():
@@ -158,19 +166,16 @@
     loads[4].start()
     for load in loads[:4]:
         load.start()
+    f_cell, c_cell = iota((1024, 256), 0), iota((1024, 256), 1)
+    c_y = c_cell // LANES * 8 + (-(c_cell // EDGE) & 7)
+    to_coarse = jnp.where(
+        (f_cell // 64 == c_y) & (f_cell % 32 // 2 == c_cell % 16), 0.125, 0.0
+    ).astype(jnp.bfloat16)
     greetings = alike + jnp.where(first, 0, 1) + jnp.where(last, n, 0)
 
     @pl.when(greetings > 0)
     def _():
         pl.semaphore_wait(barrier, greetings)
-
-    def say_entered(xy):
-        pl.semaphore_signal(entered.at[me], inc=1, device_id=(xy, z), device_id_type=MESH)
-
-    @pl.when(my_rank > 0)
-    def _():
-        for xy, its_rank in peers:
-            pl.when(its_rank < my_rank)(functools.partial(say_entered, xy))
 
     def remote(src, dst, sent, got, xy, gz):
         return pltpu.make_async_remote_copy(
@@ -193,15 +198,18 @@
         up_xy.start()
         up_z.start()
 
+    def say_entered(xy):
+        pl.semaphore_signal(entered.at[me], inc=1, device_id=(xy, z), device_id_type=MESH)
+
+    @pl.when(my_rank > 0)
+    def _():
+        for xy, its_rank in peers:
+            pl.when(its_rank < my_rank)(functools.partial(say_entered, xy))
+
     @pl.when(jnp.logical_not(first))
     def _():
         down.start()
 
-    f_cell, c_cell = iota((1024, 256), 0), iota((1024, 256), 1)
-    c_y = c_cell // LANES * 8 + (-(c_cell // EDGE) & 7)
-    to_coarse = jnp.where(
-        (f_cell // 64 == c_y) & (f_cell % 32 // 2 == c_cell % 16), 0.125, 0.0
-    ).astype(jnp.bfloat16)
     loads[0].wait()
     own_row = own[...]
     ids_send[...] = jnp.full((1, LANES), -1, jnp.int32)
@@ -331,14 +339,16 @@
     def _():
         down.wait_recv()
 
-    def make_force(k):
+    def across(k):
         b = [field[c, k] for c in range(3)]
         along_x = [shift_x(b[c]) for c in range(3)]
         along_y = [
             shift_y(b[c], by[0, 2 * c + k : 2 * c + k + 1, :], by[1, 2 * c + k : 2 * c + k + 1, :])
             for c in range(3)
         ]
-
+        return b, along_x, along_y
+
+    def make_force(k, b, along_x, along_y):
         def along_z(c):
             return (bz[1, c], field[c, 0]) if k else (field[c, 1], bz[0, c])
 
@@ -364,14 +374,15 @@
             )
             mag_new[c, k] = b[c] + 0.05 * lap
 
-    make_force(1)
+    make_force(1, *across(1))
+    prepared = across(0)
     up_xy.wait_recv()
 
     @pl.when(first)
     def _():
         down.start()
 
-    make_force(0)
+    make_force(0, *prepared)
 
     @pl.when(jnp.logical_not(first))
     def _():
@@ -405,6 +416,26 @@
             fine[c, 2 * k + 1] += gain
 
     def finish():
+        down2.wait_recv()
+        for edge in edges2:
+            edge.wait_recv()
+
+        def dz(c, k):
+            return (emf[1, c] if k == 0 else ez[1, c] - emf[0, c]) * 0.5
+
+        def dy(c, k):
+            i = 2 * (c // 2) + k
+            return central(shift_y(emf[k, c], ey[0, i : i + 1, :], ey[1, i : i + 1, :]))
+
+        def dx(c, k):
+            return central(shift_x(emf[k, c]))
+
+        for k in range(2):
+            mag_new[0, k] += 0.1 * (dy(2, k) - dz(1, k))
+            mag_new[1, k] += 0.1 * (dz(0, k) - dx(2, k))
+            mag_new[2, k] += 0.1 * (dx(1, k) - dy(0, k))
+
+    def finish_below():
         @pl.when(jnp.logical_not(first))
         def _():
             up2.wait_recv()
@@ -418,27 +449,12 @@
             for c in range(2):
                 ez[0, c] = e[c]
 
-        down2.wait_recv()
-        for edge in edges2:
-            edge.wait_recv()
-
-        def dz(c, k):
-            return central((emf[1, c], ez[0, c]) if k == 0 else (ez[1, c], emf[0, c]))
-
-        def dy(c, k):
-            i = 2 * (c // 2) + k
-            return central(shift_y(emf[k, c], ey[0, i : i + 1, :], ey[1, i : i + 1, :]))
-
-        def dx(c, k):
-            return central(shift_x(emf[k, c]))
-
-        for k in range(2):
-            mag_new[0, k] += 0.1 * (dy(2, k) - dz(1, k))
-            mag_new[1, k] += 0.1 * (dz(0, k) - dx(2, k))
-            mag_new[2, k] += 0.1 * (dx(1, k) - dy(0, k))
+        mag_new[0, 0] += 0.05 * ez[0, 1]
+        mag_new[1, 0] -= 0.05 * ez[0, 0]
 
     update(1)
     finish()
+    finish_below()
     update(0)
 
     for edge in [up_xy, up_z, down, down2, *edges, *edges2]:

time: 30.1 us -> 29.9 us (level)
  no operation moved by 1% of the time
where the time goes in v5:
time: 29.9 us; the launch traced here: 29.7 us
  Pallas kernels  29.1 us (97%)
  between operations  0.64 us (2%)
    pallas_call x1, Pallas kernels, body(): pl.pallas_call(functools.partial(kernel, cols, rows, depth), out_shape=(p...  27.8 us
    pallas_call x1, Pallas kernels, body(): pl.pallas_call(write_out, out_shape=(jax.ShapeDtypeStruct(velocity.shape,...  1.26 us

profile of v5, /device:TPU:8, one launch (start us, length us, event | category | flops | bytes accessed | tf_op | source)
XLA Modules:
  0.0 29.7 jit_solution(4815748174067858085)
XLA Ops:
  0.6 27.8 %dynamo_substep.1 = (f32[3,4,32,1024]{3,2,1,0:T(8,128)S(1)}, f32[3,2,16,512]{3,2,1,0:T(8,128)S(1)}) custom-call(f32[3,4,32,1024]{3,2,1,0:T(8,128)} %vel.1, f32[3,2,16,512]{3,2,1,0:T(8,128)} %mag.1, s32[1,32]{1,0:T(1,128)} %bitcast.1), custom_call_target="tpu_custom_call" | custom-call | tf_op jit(solution)/shard_map/dynamo_substep/pallas_call | solution.py:498
  28.5 1.3 %write_out.1 = (f32[3,4,32,1024]{3,2,1,0:T(8,128)}, f32[3,2,16,512]{3,2,1,0:T(8,128)}) custom-call(f32[3,4,32,1024]{3,2,1,0:T(8,128)S(1)} %get-tuple-element.4.fine, f32[3,2,16,512]{3,2,1,0:T(8,128)S(1)} %get-tuple-element.5.mag_new), custom_call_target="tpu_custom_call" | custom-call | tf_op jit(solution)/shard_map/write_out/pallas_call | solution.py:530

commit v6 on v5

--- a/solution.py
+++ b/solution.py
@@ -92,10 +92,21 @@
     ]
 
 
+def gains(blocks, back, to_fine):
+    n = back.shape[0]
+    high, low = halves(jnp.concatenate([blocks[:, r, :] for r in range(HALF_ROWS)], axis=1))
+    parts = [dot(back, part).astype(jnp.bfloat16) for part in (high, low)]
+    wide = dot(
+        jnp.concatenate([part[:, 256 * c : 256 * c + 256] for part in parts for c in range(3)], axis=0),
+        to_fine,
+    )
+    return [wide[n * c : n * c + n] + wide[n * (3 + c) : n * (4 + c)] for c in range(3)]
+
+
 def kernel(
     cols, rows, depth,
-    vel, mag, table, fine, mag_new,
-    field, own, ids_send, ids, v_send, v_got, w_got, f_send, f_got,
+    vel, mag, table, fine, mag_new, f_got, back_out, to_fine_out,
+    field, own, ids_send, ids, v_send, v_got, w_got, f_send, f_got_1,
     by_send, by, bz, ey_send, ey, emf, ez,
     load_sems, send_sems, entered, ids_sem, v_sem, w_sem, f_sem, by_sem, bz_sems, ey_sem, ez_sems,
 ):
@@ -339,6 +350,8 @@
     def _():
         down.wait_recv()
 
+    got = (f_got, f_got_1)
+
     def across(k):
         b = [field[c, k] for c in range(3)]
         along_x = [shift_x(b[c]) for c in range(3)]
@@ -360,8 +373,8 @@
         for r in range(HALF_ROWS):
             f_send[k, :, r, :] = by_peer[:, LANES * r : LANES * r + LANES]
         for xy, _ in peers:
-            remote(f_send.at[k, xy], f_got.at[k, me], send_sems.at[5 + k], f_sem.at[k], xy, z).start()
-        f_got[k, me] = f_send[k, me]
+            remote(f_send.at[k, xy], got[k].at[me], send_sems.at[5 + k], f_sem.at[k], xy, z).start()
+        got[k][me] = f_send[k, me]
         if not k:
             up_z.wait_recv()
         for c in range(3):
@@ -402,18 +415,14 @@
         (f_cell2 // 64 == c_cell2 // 16) & (f_cell2 % 32 // 2 == c_cell2 % 16)
     ).astype(jnp.bfloat16)
 
-    def update(k):
-        wait_all(f_got.at[k], f_sem.at[k])
-        high, low = halves(jnp.concatenate([f_got[k, :, r, :] for r in range(HALF_ROWS)], axis=1))
-        parts = [dot(back, part).astype(jnp.bfloat16) for part in (high, low)]
-        wide = dot(
-            jnp.concatenate([part[:, 256 * c : 256 * c + 256] for part in parts for c in range(3)], axis=0),
-            to_fine,
-        )
-        for c in range(3):
-            gain = wide[n * c : n * c + n] + wide[n * (3 + c) : n * (4 + c)]
-            fine[c, 2 * k] += gain
-            fine[c, 2 * k + 1] += gain
+    back_out[...] = back.astype(jnp.float32)
+    to_fine_out[...] = to_fine
+
+    def update_upper():
+        wait_all(f_got_1, f_sem.at[1])
+        for c, gain in enumerate(gains(f_got_1, back, to_fine)):
+            fine[c, 2] += gain
+            fine[c, 3] += gain
 
     def finish():
         down2.wait_recv()
@@ -452,10 +461,10 @@
         mag_new[0, 0] += 0.05 * ez[0, 1]
         mag_new[1, 0] -= 0.05 * ez[0, 0]
 
-    update(1)
+    update_upper()
     finish()
     finish_below()
-    update(0)
+    wait_all(f_got, f_sem.at[0])
 
     for edge in [up_xy, up_z, down, down2, *edges, *edges2]:
         edge.wait_send()
@@ -475,15 +484,19 @@
         wait_all(f_send.at[k], send_sems.at[5 + k])
 
 
-def write_out(fine, mag_new, vel_out, mag_out, sems):
-    copies = [
-        pltpu.make_async_copy(fine.at[c, pl.ds(2 * k, 2)], vel_out.at[c, pl.ds(2 * k, 2)], sems.at[2 * c + k])
-        for c in range(3)
-        for k in range(2)
-    ]
+def write_out(fine, mag_new, f_got, back, to_fine, vel_out, mag_out, lower, sems):
+    def written(k, c, ref):
+        return pltpu.make_async_copy(ref, vel_out.at[c, pl.ds(2 * k, 2)], sems.at[3 * k + c])
+
+    copies = [written(1, c, fine.at[c, pl.ds(2, 2)]) for c in range(3)]
     copies += [pltpu.make_async_copy(mag_new, mag_out, sems.at[6])]
     for copy in copies:
         copy.start()
+    for c, gain in enumerate(gains(f_got, back[...].astype(jnp.bfloat16), to_fine[...])):
+        lower[c, 0] = fine[c, 0] + gain
+        lower[c, 1] = fine[c, 1] + gain
+        copies.append(written(0, c, lower.at[c]))
+        copies[-1].start()
     for copy in copies:
         copy.wait()
 
@@ -495,14 +508,17 @@
     far = pl.BlockSpec(memory_space=pl.ANY)
     near = pl.BlockSpec(memory_space=pltpu.VMEM)
     dma = pltpu.SemaphoreType.DMA
-    fine, mag_new = pl.pallas_call(
+    made = pl.pallas_call(
         functools.partial(kernel, cols, rows, depth),
         out_shape=(
             pltpu.VMEM(velocity.shape, f32),
             pltpu.VMEM(magnetic.shape, f32),
+            pltpu.VMEM((n, HALF_ROWS, LANES), f32),
+            pltpu.VMEM((n, n), f32),
+            pltpu.VMEM((256, 1024), jnp.bfloat16),
         ),
         in_specs=[far, far, far],
-        out_specs=(near, near),
+        out_specs=(near,) * 5,
         scratch_shapes=[
             pltpu.VMEM((3, 2, EDGE, width), f32),
             pltpu.VMEM((1, n), jnp.int32),
@@ -512,7 +528,7 @@
             pltpu.VMEM((n, ROWS, LANES), f32),
             pltpu.VMEM((n, 6, LANES), f32),
             pltpu.VMEM((2, n, HALF_ROWS, LANES), f32),
-            pltpu.VMEM((2, n, HALF_ROWS, LANES), f32),
+            pltpu.VMEM((n, HALF_ROWS, LANES), f32),
             pltpu.VMEM((2, 6, width), f32),
             pltpu.VMEM((2, 6, width), f32),
             pltpu.VMEM((2, 3, EDGE, width), f32),
@@ -533,11 +549,12 @@
             jax.ShapeDtypeStruct(velocity.shape, f32),
             jax.ShapeDtypeStruct(magnetic.shape, f32),
         ),
-        in_specs=[near, near],
+        in_specs=[near] * 5,
         out_specs=(far, far),
-        scratch_shapes=[dma((7,))],
+        scratch_shapes=[pltpu.VMEM((3, 2, n, 1024), f32), dma((7,))],
+        compiler_params=pltpu.CompilerParams(vmem_limit_bytes=16 << 20),
         name="write_out",
-    )(*(pltpu.with_memory_space_constraint(a, pltpu.VMEM) for a in (fine, mag_new)))
+    )(*(pltpu.with_memory_space_constraint(a, pltpu.VMEM) for a in made))
 
 
 def solution(mesh):

time: 29.9 us -> 29.5 us (0.987)
  Pallas kernels: 29.1 us -> 28.7 us
    pallas_call x1, Pallas kernels: 27.8 us -> 27.4 us  [body(): pl.pallas_call(functools.partial(kernel, cols, rows, depth), out_shape=(p...]
where the time goes in v6:
time: 29.5 us; the launch traced here: 29.4 us
  Pallas kernels  28.7 us (97%)
  between operations  0.64 us (2%)
    pallas_call x1, Pallas kernels, body(): pl.pallas_call(functools.partial(kernel, cols, rows, depth), out_shape=(p...  27.4 us
    pallas_call x1, Pallas kernels, body(): pl.pallas_call(write_out, out_shape=(jax.ShapeDtypeStruct(velocity.shape,...  1.32 us

profile of v6, /device:TPU:8, one launch (start us, length us, event | category | flops | bytes accessed | tf_op | source)
XLA Modules:
  0.0 29.4 jit_solution(7697118508379507722)
XLA Ops:
  0.6 27.4 %dynamo_substep.1 = (f32[3,4,32,1024]{3,2,1,0:T(8,128)S(1)}, f32[3,2,16,512]{3,2,1,0:T(8,128)S(1)}, f32[32,6,128]{2,1,0:T(8,128)S(1)}, f32[32,32]{1,0:T(8,128)S(1)}, bf16[256,1024]{1,0:T(8,128)(2,1)S(1)}) custom-call(f32[3,4,32,1024]{3,2,1,0:T(8,128)} %vel.1, f32[3,2,16,512]{3,2,1,0:T(8,128)} %mag.1, s32[1,32]{1,0:T(1,128)} %bitcast.1), custom_call_target="tpu_custom_call" | custom-call | tf_op jit(solution)/shard_map/dynamo_substep/pallas_call | solution.py:511
  28.1 1.3 %write_out.1 = (f32[3,4,32,1024]{3,2,1,0:T(8,128)}, f32[3,2,16,512]{3,2,1,0:T(8,128)}) custom-call(f32[3,4,32,1024]{3,2,1,0:T(8,128)S(1)} %get-tuple-element.7.fine, f32[3,2,16,512]{3,2,1,0:T(8,128)S(1)} %get-tuple-element.8.mag_new, f32[32,6,128]{2,1,0:T(8,128)S(1)} %get-tuple-element.9.f_got, f32[32,32]{1,0:T(8,128)S(1)} %get-tuple-element.10.back, ...), custom_call_target="tpu_custom_call" | custom-call | tf_op jit(solution)/shard_map/write_out/pallas_call | solution.py:546

commit v7 on v6

--- a/solution.py
+++ b/solution.py
@@ -157,7 +157,7 @@
     @pl.when(last)
     def _():
         places = [x * rows + y for y in (*range(rows // 2), *range(rows - 1, rows // 2 - 1, -1)) for x in range(cols)]
-        for q in range(1, n):
+        for q in range(n - 1, 0, -1):
             pl.when(q > my_rank)(functools.partial(greet, places[q], z))
 
     @pl.when(jnp.logical_not(jnp.logical_or(last, my_rank > 0)))

time: 29.5 us -> 29.5 us (level)
  no operation moved by 1% of the time
where the time goes in v7:
time: 29.5 us; the launch traced here: 29.3 us
  Pallas kernels  28.7 us (97%)
  between operations  0.64 us (2%)
    pallas_call x1, Pallas kernels, body(): pl.pallas_call(functools.partial(kernel, cols, rows, depth), out_shape=(p...  27.4 us
    pallas_call x1, Pallas kernels, body(): pl.pallas_call(write_out, out_shape=(jax.ShapeDtypeStruct(velocity.shape,...  1.32 us

profile of v7, /device:TPU:8, one launch (start us, length us, event | category | flops | bytes accessed | tf_op | source)
XLA Modules:
  0.0 29.3 jit_solution(7722437539804199696)
XLA Ops:
  0.6 27.4 %dynamo_substep.1 = (f32[3,4,32,1024]{3,2,1,0:T(8,128)S(1)}, f32[3,2,16,512]{3,2,1,0:T(8,128)S(1)}, f32[32,6,128]{2,1,0:T(8,128)S(1)}, f32[32,32]{1,0:T(8,128)S(1)}, bf16[256,1024]{1,0:T(8,128)(2,1)S(1)}) custom-call(f32[3,4,32,1024]{3,2,1,0:T(8,128)} %vel.1, f32[3,2,16,512]{3,2,1,0:T(8,128)} %mag.1, s32[1,32]{1,0:T(1,128)} %bitcast.1), custom_call_target="tpu_custom_call" | custom-call | tf_op jit(solution)/shard_map/dynamo_substep/pallas_call | solution.py:511
  28.0 1.3 %write_out.1 = (f32[3,4,32,1024]{3,2,1,0:T(8,128)}, f32[3,2,16,512]{3,2,1,0:T(8,128)}) custom-call(f32[3,4,32,1024]{3,2,1,0:T(8,128)S(1)} %get-tuple-element.7.fine, f32[3,2,16,512]{3,2,1,0:T(8,128)S(1)} %get-tuple-element.8.mag_new, f32[32,6,128]{2,1,0:T(8,128)S(1)} %get-tuple-element.9.f_got, f32[32,32]{1,0:T(8,128)S(1)} %get-tuple-element.10.back, ...), custom_call_target="tpu_custom_call" | custom-call | tf_op jit(solution)/shard_map/write_out/pallas_call | solution.py:546
